TPU v7x, 256 devices: a whole 4x4x8 slice. The times are simulated.
256 devices in a mesh: ctx: 32 (over x, y, core), tp: 8 (over z).
Axes of the slice: x: 4, y: 4, z: 8, core: 2. Of those that a mesh axis runs over, the one named last changes fastest.
Arguments:
- x_first: bfloat16 [32, 8192], P(None, 'ctx')
- x_second: bfloat16 [32, 8192], P(None, 'ctx')
- norm_gain: bfloat16 [8192], P('ctx'), may hold values from 0.099609375 to 1.8984375
- w_query: bfloat16 [8192, 8192], P('ctx', 'tp')
- key_value_weight: bfloat16 [8192, 2048], P('ctx', 'tp')
- w_out: bfloat16 [8192, 8192], P('tp', 'ctx'), may hold values from -0.125 to 0.125
- key_cache: bfloat16 [1376, 128, 1024], P('ctx', None, 'tp')
- value_cache: bfloat16 [1376, 128, 1024], P('ctx', None, 'tp'), may hold values from -12 to 12
- lengths: int32 [32], replicated, may hold values from 128 to 16384, as said below
- page_table: int32 [32, 128], replicated, may hold values from -1 to 1375, as said below
- move_from: int32 [64], replicated, may hold values from 0 to 1375, as said below
- move_to: int32 [64], replicated, may hold values from 0 to 1375, as said below
Outputs:
- out_first: bfloat16 [32, 8192], P('tp', 'ctx')
- out_second: bfloat16 [32, 8192], P('tp', 'ctx')
- moved_k: bfloat16 [1376, 128, 1024], P('ctx', None, 'tp')
- moved_v: bfloat16 [1376, 128, 1024], P('ctx', None, 'tp')
Inputs may be any that keep to these rules, and one draw needn't show every extreme that they name: `lengths`: one request has exactly 16384 cached tokens; every other has fewer than 8192. `page_table`: entry (r, p) is shard * 43 + slot for p < ceil(lengths[r] / 128) and -1 after; no global slot appears twice; the pages of a shard fill its slots from 0 upwards and stay below slot 35, which some shard fills completely. `move_from`: entries 2 * c to 2 * c + 1 are distinct slots of shard c that appear in page_table. `move_to`: distinct slots, each at or above slot 35 of its shard; the 2 pages that one shard gives up go to 2 different shards; a receiving shard gets exactly 8 pages.
All inputs are finite; a program needn't handle non-finite values.
Results may differ from a plain program's by a relative error of at most 0.018.
Values may be sent and summed in bfloat16 or wider, within the bound.
A program may use at most 64 MiB of HBM per device.

v0:
```python
import jax
import jax.numpy as jnp
from jax import lax
from jax.sharding import PartitionSpec as P

MODEL_WIDTH = 8192
QUERY_HEADS = 64
KEY_VALUE_HEADS = 8
HEAD_SIZE = 128
PAGE_TOKENS = 128
REQUEST_PAGES = 128


THETA = 500000.0
EPSILON = 1e-05
NEGATIVE = -1e30


def combined_all(x, axis, combine):
    everything = jax.tree.map(lambda part: lax.all_gather(part, axis), x)
    initial = jax.tree.map(lambda part: part[0], everything)

    def lap(k, so_far):
        return combine(so_far, jax.tree.map(lambda part: part[k], everything))

    return lax.fori_loop(1, lax.axis_size(axis), lap, initial)


def rotate(vectors, positions):
    half_dim = HEAD_SIZE // 2
    inverse = THETA ** (-(jnp.arange(half_dim, dtype=jnp.float32) * 2.0 / HEAD_SIZE))
    angles = positions.astype(jnp.float32)[:, None] * inverse[None, :]
    cosine = jnp.cos(angles)[:, None, :]
    sine_part = jnp.sin(angles)[:, None, :]
    first_half = vectors[..., :half_dim]
    second_half = vectors[..., half_dim:]
    return jnp.concatenate(
        [
            first_half * cosine - second_half * sine_part,
            second_half * cosine + first_half * sine_part,
        ],
        axis=-1,
    )


def combine_parts(earlier, later):
    peak_score = jnp.maximum(earlier[0], later[0])
    first_scale = jnp.exp(earlier[0] - peak_score)
    second_scale = jnp.exp(later[0] - peak_score)
    return (
        peak_score,
        earlier[1] * first_scale + later[1] * second_scale,
        earlier[2] * first_scale[..., None] + later[2] * second_scale[..., None],
    )


def project_local(inputs, norm_gain, w_query, key_value_weight, positions):
    widened = inputs.astype(jnp.float32)
    squares = jnp.sum(widened * widened, axis=1)
    scaled = (widened * norm_gain.astype(jnp.float32)[None, :]).astype(jnp.bfloat16)
    query_portion = jnp.dot(scaled, w_query, preferred_element_type=jnp.float32)
    keyval_part = jnp.dot(scaled, key_value_weight, preferred_element_type=jnp.float32)
    squares, query_portion, keyval_part = lax.psum((squares, query_portion, keyval_part), "ctx")
    inverse_root_mean = lax.rsqrt(squares / MODEL_WIDTH + EPSILON)
    count_of_rows = inputs.shape[0]
    shard_heads = key_value_weight.shape[1] // (2 * HEAD_SIZE)
    queries = rotate(
        (query_portion * inverse_root_mean[:, None]).reshape(
            count_of_rows, shard_heads * (QUERY_HEADS // KEY_VALUE_HEADS), HEAD_SIZE
        ),
        positions,
    ).astype(jnp.bfloat16)
    key_value_pair = (keyval_part * inverse_root_mean[:, None]).reshape(
        count_of_rows, shard_heads, 2, HEAD_SIZE
    )
    new_keys = rotate(key_value_pair[:, :, 0], positions).astype(jnp.bfloat16)
    return (queries, new_keys, key_value_pair[:, :, 1].astype(jnp.bfloat16))


def collect_blocks(member, owner_row, block_max, block_total, block_out, request_max):
    slot_count = block_max.shape[0]
    block_scale = jnp.exp(block_max - request_max[owner_row])
    member_matrix = member.astype(jnp.float32)
    totals = jnp.einsum(
        "rs,skg->rkg", member_matrix, block_total * block_scale, precision=lax.Precision.HIGHEST
    )
    outputs = jnp.dot(
        member_matrix,
        (block_out * block_scale[..., None]).reshape(slot_count, -1),
        precision=lax.Precision.HIGHEST,
        preferred_element_type=jnp.float32,
    )
    return (totals, outputs.reshape((member.shape[0],) + block_out.shape[1:]))


def attend_local(queries, new_keys, new_values, page_table, lengths, k_local, v_local):
    slot_count = k_local.shape[0]
    shard_heads = k_local.shape[2] // HEAD_SIZE
    query_group_size = QUERY_HEADS // KEY_VALUE_HEADS
    requests = queries.shape[0]
    score_scale = HEAD_SIZE ** (-0.5)
    global_ids = lax.axis_index("ctx") * slot_count + jnp.arange(slot_count, dtype=jnp.int32)
    flat_table = page_table.reshape(-1)
    matches = flat_table[None, :] == global_ids[:, None]
    present = jnp.any(matches, axis=1)
    flat_index = jnp.sum(
        jnp.where(matches, jnp.arange(flat_table.shape[0], dtype=jnp.int32)[None, :], 0), axis=1
    )
    owner_row = flat_index // REQUEST_PAGES
    page_index = flat_index % REQUEST_PAGES
    slot_queries = queries[owner_row].reshape(slot_count, shard_heads, query_group_size, HEAD_SIZE)
    keys_of_page = k_local.reshape(slot_count, PAGE_TOKENS, shard_heads, HEAD_SIZE)
    values_of_page = v_local.reshape(slot_count, PAGE_TOKENS, shard_heads, HEAD_SIZE)
    scores = (
        jnp.einsum(
            "skgd,spkd->skgp", slot_queries, keys_of_page, preferred_element_type=jnp.float32
        )
        * score_scale
    )
    positions = (
        page_index[:, None] * PAGE_TOKENS + jnp.arange(PAGE_TOKENS, dtype=jnp.int32)[None, :]
    )
    is_valid = (present[:, None] & (positions < lengths[owner_row][:, None]))[:, None, None, :]
    scores = jnp.where(is_valid, scores, NEGATIVE)
    block_max = jnp.max(scores, axis=-1)
    weights = jnp.where(is_valid, jnp.exp(scores - block_max[..., None]), 0.0).astype(jnp.bfloat16)
    block_total = jnp.sum(weights.astype(jnp.float32), axis=-1)
    block_out = jnp.einsum(
        "skgp,spkd->skgd", weights, values_of_page, preferred_element_type=jnp.float32
    )
    member = (owner_row[None, :] == jnp.arange(requests, dtype=jnp.int32)[:, None]) & present[
        None, :
    ]
    local_max = jnp.max(jnp.where(member[:, :, None, None], block_max[None], NEGATIVE), axis=1)
    totals, outputs = collect_blocks(
        member, owner_row, block_max, block_total, block_out, local_max
    )
    request_max, totals, outputs = combined_all((local_max, totals, outputs), "ctx", combine_parts)
    grouped_queries = queries.reshape(requests, shard_heads, query_group_size, HEAD_SIZE)
    own_scores = (
        jnp.einsum("rkgd,rnkd->rkgn", grouped_queries, new_keys, preferred_element_type=jnp.float32)
        * score_scale
    )
    own_max = jnp.max(own_scores, axis=-1)
    own_weights = jnp.exp(own_scores - own_max[..., None]).astype(jnp.bfloat16)
    own_total = jnp.sum(own_weights.astype(jnp.float32), axis=-1)
    own_out = jnp.einsum(
        "rkgn,rnkd->rkgd", own_weights, new_values, preferred_element_type=jnp.float32
    )
    peak_score = jnp.maximum(request_max, own_max)
    far_scale = jnp.exp(request_max - peak_score)
    near_scale = jnp.exp(own_max - peak_score)
    numerator = outputs * far_scale[..., None] + own_out * near_scale[..., None]
    denominator = totals * far_scale + own_total * near_scale
    return (numerator / denominator[..., None]).reshape(requests, -1).astype(jnp.bfloat16)


def mix_heads(inputs, attention, w_out):
    count_of_rows = inputs.shape[0] // lax.axis_size("tp")
    summed = lax.psum_scatter(
        jnp.dot(attention, w_out, preferred_element_type=jnp.float32),
        "tp",
        scatter_dimension=0,
        tiled=True,
    )
    residual = lax.dynamic_slice_in_dim(
        inputs, lax.axis_index("tp") * count_of_rows, count_of_rows, 0
    )
    return (residual.astype(jnp.float32) + summed).astype(jnp.bfloat16)


def retable(page_table, move_from, move_to):
    matches = page_table[:, :, None] == move_from[None, None, :]
    target = jnp.sum(jnp.where(matches, move_to[None, None, :], 0), axis=-1)
    return jnp.where(jnp.any(matches, axis=-1), target, page_table)


def per_device(
    x_first,
    x_second,
    norm_gain,
    w_query,
    key_value_weight,
    w_out,
    key_cache,
    value_cache,
    lengths,
    page_table,
    move_from,
    move_to,
):
    slot_count = key_cache.shape[0]
    shard_index = lax.axis_index("ctx")
    shard_total = lax.axis_size("ctx")
    first_query, first_key, first_value = project_local(
        x_first, norm_gain, w_query, key_value_weight, lengths
    )
    first_attention = attend_local(
        first_query,
        first_key[:, None],
        first_value[:, None],
        page_table,
        lengths,
        key_cache,
        value_cache,
    )
    out_first = mix_heads(x_first, first_attention, w_out)
    per_shard = move_from.shape[0] // shard_total
    own_from = (
        lax.dynamic_slice_in_dim(move_from, shard_index * per_shard, per_shard)
        - shard_index * slot_count
    )
    own_to = lax.dynamic_slice_in_dim(move_to, shard_index * per_shard, per_shard)
    leaving_k = key_cache[own_from]
    leaving_v = value_cache[own_from]
    global_ids = shard_index * slot_count + jnp.arange(slot_count, dtype=jnp.int32)
    departed = jnp.any(move_from[None, :] == global_ids[:, None], axis=1)[:, None, None]
    kept_k = jnp.where(departed, jnp.zeros((), jnp.bfloat16), key_cache)
    kept_v = jnp.where(departed, jnp.zeros((), jnp.bfloat16), value_cache)
    piece_k = lax.all_gather(leaving_k, "ctx", axis=0, tiled=True)
    piece_v = lax.all_gather(leaving_v, "ctx", axis=0, tiled=True)
    piece_to = lax.all_gather(own_to, "ctx", axis=0, tiled=True)
    placing = piece_to[None, :] == global_ids[:, None]
    arrived = jnp.any(placing, axis=1)[:, None, None]
    placing_matrix = placing.astype(jnp.bfloat16)
    placed_k = jnp.einsum(
        "sn,npw->spw", placing_matrix, piece_k, preferred_element_type=jnp.float32
    ).astype(jnp.bfloat16)
    placed_v = jnp.einsum(
        "sn,npw->spw", placing_matrix, piece_v, preferred_element_type=jnp.float32
    ).astype(jnp.bfloat16)
    moved_k = jnp.where(arrived, placed_k, kept_k)
    moved_v = jnp.where(arrived, placed_v, kept_v)
    second_query, second_key, second_value = project_local(
        x_second, norm_gain, w_query, key_value_weight, lengths + 1
    )
    keys_both = jnp.stack([first_key, second_key], axis=1)
    values_both = jnp.stack([first_value, second_value], axis=1)
    table_after = retable(page_table, move_from, move_to)
    second_attention = attend_local(
        second_query, keys_both, values_both, table_after, lengths, moved_k, moved_v
    )
    out_second = mix_heads(x_second, second_attention, w_out)
    return (out_first, out_second, moved_k, moved_v)


def solution(mesh):
    in_specs = (
        P(None, "ctx"),
        P(None, "ctx"),
        P("ctx"),
        P("ctx", "tp"),
        P("ctx", "tp"),
        P("tp", "ctx"),
        P("ctx", None, "tp"),
        P("ctx", None, "tp"),
        P(),
        P(),
        P(),
        P(),
    )
    out_specs = (P("tp", "ctx"), P("tp", "ctx"), P("ctx", None, "tp"), P("ctx", None, "tp"))
    return jax.shard_map(
        per_device, mesh=mesh, in_specs=in_specs, out_specs=out_specs, check_vma=False
    )
```

profile of v0, /device:TPU:1, one launch (start us, length us, event | category | flops | bytes accessed | tf_op | source)
XLA Modules:
  0.0 598.4 jit_solution(4843836035880479083)
XLA Ops:
  8.1 1.3 fusion.50
  9.4 1.3 fusion.52
  10.7 1.7 fusion.99
  12.4 1.7 fusion.95
  14.2 1.6 fusion.101
  15.8 1.6 fusion.97
  18.8 2.5 gather_fusion.7
  26.0 99.4 %all-reduce.10.cloned.1.call-done = (f32[32]{0:T(128)}, f32[32,256]{1,0:T(8,128)}, f32[32]{0:T(128)}, f32[32,256]{1,0:T(8,128)}) async-done(((f32[32]{0:T(128)}, f32[32,256]{1,0:T(8,128)}, f32[32]{0:T(128)}, f32[32,256]{1,0:T(8,128)}), (f32[32]{0:T(128)}, f32[32,256]{1,0:T(8,128)}, f32[32]{0:T(128)}, f32[32,256]{1,0:T(8,128)})) %all-reduce.10.cloned.1.call-update) | async-done | bytes 65808 | tf_op jit(solution)/shard_map/psum | solution.py:63
  126.8 112.5 %all-reduce.12.cloned.1.call-done = (f32[32,1024]{1,0:T(8,128)}, f32[32,1024]{1,0:T(8,128)}) async-done(((f32[32,1024]{1,0:T(8,128)}, f32[32,1024]{1,0:T(8,128)}), (f32[32,1024]{1,0:T(8,128)}, f32[32,1024]{1,0:T(8,128)})) %all-reduce.12.cloned.1.call-update) | async-done | bytes 262160 | tf_op jit(solution)/shard_map/psum | solution.py:63
  239.3 1.7 multiply_bitcast_fusion
  243.2 2.4 fusion.134
  250.0 1.6 fusion.39
  253.2 1.3 dynamic-slice
  256.0 13.0 %all-reduce = s32[64]{0:T(128)S(1)} all-reduce(s32[64]{0:T(128)S(1)} %dynamic-slice_dynamic-update-slice_fusion), channel_id=1, replica_groups=mesh['ctx'=32,'tp'=8] {'ctx'}, use_global_device_ids=true, to_apply=%add | all-reduce | flops 64 | bytes 512
  275.1 27.0 %all-gather.8 = f32[32,32,8]{1,2,0:T(8,128)S(1)} all-gather(f32[1,32,8]{1,2,0:T(8,128)S(1)} %copy.256), channel_id=2, replica_groups=mesh['ctx'=32,'tp'=8] {'ctx'}, dimensions={0}, use_global_device_ids=true | all-gather | bytes 33792 | tf_op jit(solution)/shard_map/all_gather | solution.py:20
  302.6 22.1 %all-gather.9 = f32[32,32,8]{1,2,0:T(8,128)S(1)} all-gather(f32[1,32,8]{1,2,0:T(8,128)S(1)} %convolution_bitcast_fusion.1), channel_id=3, replica_groups=mesh['ctx'=32,'tp'=8] {'ctx'}, dimensions={0}, use_global_device_ids=true | all-gather | bytes 33792 | tf_op jit(solution)/shard_map/all_gather | solution.py:20
  325.5 3.9 fusion.23
  331.8 9.8 %all-gather.21.cloned.1.call-done = bf16[64,128,128]{2,1,0:T(8,128)(2,1)} async-done(((bf16[2,128,128]{2,1,0:T(8,128)(2,1)}), bf16[64,128,128]{2,1,0:T(8,128)(2,1)}) %all-gather.21.cloned.1.call-update) | async-done | bytes 2097168 | tf_op jit(solution)/shard_map/all_gather | solution.py:221
  341.6 4.3 fusion.22
  346.3 23.9 %all-gather.10 = f32[32,32,8]{1,2,0:T(8,128)S(1)} all-gather(f32[1,32,8]{1,2,0:T(8,128)S(1)} %copy.272), channel_id=6, replica_groups=mesh['ctx'=32,'tp'=8] {'ctx'}, dimensions={0}, use_global_device_ids=true | all-gather | bytes 33792 | tf_op jit(solution)/shard_map/all_gather | solution.py:20
  370.6 22.5 %all-gather.11 = f32[32,32,8]{1,2,0:T(8,128)S(1)} all-gather(f32[1,32,8]{1,2,0:T(8,128)S(1)} %convolution_bitcast_fusion), channel_id=7, replica_groups=mesh['ctx'=32,'tp'=8] {'ctx'}, dimensions={0}, use_global_device_ids=true | all-gather | bytes 33792 | tf_op jit(solution)/shard_map/all_gather | solution.py:20
  395.8 82.8 %while.38 = (s32[]{:T(128)}, f32[32,1,8]{0,2,1:T(8,128)S(1)}, f32[32,1,8]{0,2,1:T(8,128)S(1)}, f32[32,1,8,128]{3,2,1,0:T(8,128)S(1)}, f32[32,32,1,8]{1,3,2,0:T(8...) while((s32[]{:T(128)}, f32[32,1,8]{0,2,1:T(8,128)S(1)}, ...), condition=%wide.region_9.10_spmd, body=%wide.region_8.9_spmd.sunk | while | flops 100101 | bytes 674971 | solution.py:26
  480.9 41.2 %while.39 = (s32[]{:T(128)}, f32[32,1,8]{0,2,1:T(8,128)S(1)}, f32[32,1,8]{0,2,1:T(8,128)S(1)}, f32[32,1,8,128]{3,2,1,0:T(8,128)S(1)}, f32[32,32,1,8]{1,3,2,0:T(8...) while((s32[]{:T(128)}, f32[32,1,8]{0,2,1:T(8,128)S(1)}, ...), condition=%wide.region_25.26_spmd, body=%wide.region_24.25_spmd.sunk | while | flops 100101 | bytes 674971 | solution.py:26
  524.7 64.3 %all-reduce.14.cloned.1.call-done = (f32[32,256]{1,0:T(8,128)}, f32[32,256]{1,0:T(8,128)}) async-done(((f32[32,256]{1,0:T(8,128)}, f32[32,256]{1,0:T(8,128)}), (f32[32,256]{1,0:T(8,128)}, f32[32,256]{1,0:T(8,128)})) %all-reduce.14.cloned.1.call-update) | async-done | bytes 65552
  (654 shorter events, 158.0 us)
Async XLA Ops:
  7.2 118.2 %all-reduce.10.cloned.1.call-start = ((), (), s32[]{:S(2)}) async-start(), calls=%async_computation.4 | async-start | bytes 133120 | tf_op jit(solution)/shard_map/psum | solution.py:63
  14.1 225.2 %all-reduce.12.cloned.1.call-start = ((), (), s32[]{:S(2)}) async-start(), calls=%async_computation.5 | async-start | bytes 524288 | tf_op jit(solution)/shard_map/psum | solution.py:63
  17.4 307.7 %all-gather.19.cloned.1.call-start = ((), (), s32[]{:S(2)}) async-start(), calls=%async_computation.1 | async-start | bytes 2162688 | tf_op jit(solution)/shard_map/all_gather | solution.py:220
  18.7 322.8 %all-gather.21.cloned.1.call-start = ((), (), s32[]{:S(2)}) async-start(), calls=%async_computation.2 | async-start | bytes 2162688 | tf_op jit(solution)/shard_map/all_gather | solution.py:221
  21.3 373.5 %all-gather.17.cloned.1.call-start = ((), (), s32[]{:S(2)}) async-start(), calls=%async_computation | async-start | bytes 4325376 | tf_op jit(solution)/shard_map/all_gather | solution.py:20
  21.4 219.6 %copy-start.32 = (s32[43]{0:T(128)}, s32[43]{0:T(128)S(1)}, u32[]{:S(2)}) copy-start(s32[43]{0:T(128)S(1)} %iota_add_fusion) | copy-start | bytes 520
  22.9 218.4 %copy-start.31 = (s32[1024]{0:T(1024)}, s32[1024]{0:T(1024)S(1)}, u32[]{:S(2)}) copy-start(s32[1024]{0:T(1024)S(1)} %pad_clamp_fusion.2) | copy-start | bytes 12292
  23.7 217.3 %copy-start.35 = (f32[64]{0:T(128)}, f32[64]{0:T(128)S(1)}, u32[]{:S(2)}) copy-start(f32[64]{0:T(128)S(1)} %negate_power_fusion) | copy-start | bytes 772
  24.6 221.1 %copy-start.23 = (pred[43]{0:T(512)(128)(4,1)}, pred[43]{0:T(512)(128)(4,1)S(1)}, u32[]{:S(2)}) copy-start(pred[43]{0:T(512)(128)(4,1)S(1)} %get-tuple-element.493) | copy-start | bytes 133
  24.6 216.4 %copy-start.37 = (f32[32]{0:T(128)}, f32[32]{0:T(128)S(1)}, u32[]{:S(2)}) copy-start(f32[32]{0:T(128)S(1)} %get-tuple-element.568) | copy-start | bytes 388
  24.6 216.4 %copy-start.39 = (f32[32]{0:T(128)}, f32[32]{0:T(128)S(1)}, u32[]{:S(2)}) copy-start(f32[32]{0:T(128)S(1)} %get-tuple-element.569) | copy-start | bytes 388
  25.1 215.9 %copy-start.27 = (s32[43]{0:T(128)}, s32[43]{0:T(128)S(1)}, u32[]{:S(2)}) copy-start(s32[43]{0:T(128)S(1)} %get-tuple-element.579) | copy-start | bytes 520
  126.1 114.9 %copy-start.42 = (f32[32]{0:T(128)}, f32[32]{0:T(128)S(1)}, u32[]{:S(2)}) copy-start(f32[32]{0:T(128)S(1)} %add_rsqrt_fusion) | copy-start | bytes 388
  126.8 114.3 %copy-start.43 = (f32[32]{0:T(128)}, f32[32]{0:T(128)S(1)}, u32[]{:S(2)}) copy-start(f32[32]{0:T(128)S(1)} %add_rsqrt_fusion.1) | copy-start | bytes 388
  250.0 52.2 %copy-start.7 = (f32[43,8]{1,0:T(8,128)S(1)}, f32[43,8]{1,0:T(8,128)}, u32[]{:S(2)}) copy-start(f32[43,8]{1,0:T(8,128)} %get-tuple-element.572) | copy-start | bytes 4132
  251.7 50.7 %copy-start.25 = (pred[43]{0:T(512)(128)(4,1)S(1)}, pred[43]{0:T(512)(128)(4,1)}, u32[]{:S(2)}) copy-start(pred[43]{0:T(512)(128)(4,1)} %copy-done.23) | copy-start | bytes 133
  251.7 50.7 %copy-start.28 = (s32[43]{0:T(128)S(1)}, s32[43]{0:T(128)}, u32[]{:S(2)}) copy-start(s32[43]{0:T(128)} %copy-done.27) | copy-start | bytes 520
  251.7 228.2 %all-gather.23.cloned.1.call-start = ((), (), s32[]{:S(2)}) async-start(), calls=%async_computation.3 | async-start | bytes 4325376 | tf_op jit(solution)/shard_map/all_gather | solution.py:20
  253.2 72.4 %copy-start.33 = (s32[43]{0:T(128)S(1)}, s32[43]{0:T(128)}, u32[]{:S(2)}) copy-start(s32[43]{0:T(128)} %copy-done.32) | copy-start | bytes 520
  269.0 56.1 %copy-start.44 = (s32[64]{0:T(128)}, s32[64]{0:T(128)S(1)}, u32[]{:S(2)}) copy-start(s32[64]{0:T(128)S(1)} %all-reduce) | copy-start | bytes 772
  269.8 55.2 %copy-start.46 = (pred[43]{0:T(512)(128)(4,1)}, pred[43]{0:T(512)(128)(4,1)S(1)}, u32[]{:S(2)}) copy-start(pred[43]{0:T(512)(128)(4,1)S(1)} %get-tuple-element.494) | copy-start | bytes 133
  269.8 55.2 %copy-start.48 = (pred[43]{0:T(512)(128)(4,1)}, pred[43]{0:T(512)(128)(4,1)S(1)}, u32[]{:S(2)}) copy-start(pred[43]{0:T(512)(128)(4,1)S(1)} %get-tuple-element.495) | copy-start | bytes 133
  394.6 194.3 %all-reduce.14.cloned.1.call-start = ((), (), s32[]{:S(2)}) async-start(), calls=%async_computation.6 | async-start | bytes 131072
  395.8 83.3 %copy-start.4 = (bf16[1024,256]{1,0:T(8,128)(2,1)S(1)}, bf16[1024,256]{1,0:T(8,128)(2,1)}, u32[]{:S(2)}) copy-start(bf16[1024,256]{1,0:T(8,128)(2,1)} %param.21) | copy-start | bytes 1572868
  (34 other events, 654.7 us)
Sparse Core Ops, SparseCore 0:
  14.3 111.1 all-reduce.9
  129.6 109.6 all-reduce.11
  241.9 48.9 all-gather.18
  293.2 48.2 all-gather.20
  344.1 50.6 all-gather.16
  397.3 50.3 all-gather.22
  523.5 65.3 all-reduce.13
where the time goes:
time: 607 us; the launch traced here: 598 us
  waiting for transfers between devices  286 us (47%)
  blocking collectives  108 us (18%)
  local copies, waits for them, and re-layouts  85.2 us (14%)
  other arithmetic  74.2 us (12%)
  matrix products  25 us (4%)
  between operations  16.4 us (3%)
    psum x2, waiting for transfers between devices, project_local(): lax.psum((squares, query_portion, keyval_part), 'ctx')  212 us
    all_gather x4, blocking collectives, combined_all(): everything = jax.tree.map(lambda part: lax.all_gather(part, axis), x)  95.5 us
    unnamed x8, waiting for transfers between devices  64.4 us
    dynamic_slice x62, local copies, waits for them, and re-layouts, lap(): return combine(so_far, jax.tree.map(lambda part: part[k], everything))  57.4 us
    mul x62, other arithmetic, combine_parts(): later[2] * second_scale[..., None]  22.2 us
    mul x62, other arithmetic, combine_parts(): earlier[2] * first_scale[..., None] + later[2] * second_scale[..., None]  21.8 us
    unnamed x1, blocking collectives  13 us
  transfers between devices with their start and end apart: 7, of which 5 were waited for; matrix products, arithmetic and copies ran while one was open for 22% of the time, Pallas kernels for 0%

commit v1 on v0

v1 whole, which is shorter than its diff:
```python
import functools

import jax
import jax.numpy as jnp
import numpy as np
from jax import lax
from jax.experimental import pallas as pl
from jax.experimental.pallas import tpu as pltpu
from jax.sharding import PartitionSpec as P

HEAD = 128
GROUP = 8
PAGE = 128
ARRIVALS = 8
THETA = 500000.0
EPSILON = 1e-05
NEGATIVE = -1e30
SCALE = HEAD**-0.5
MESH = pl.DeviceIdType.MESH
F32 = jnp.float32
BF16 = jnp.bfloat16

TURN_HIGH = 6.28125
TURN_MID = float(np.float32(np.round((2 * np.pi - TURN_HIGH) * 2.0**20) / 2.0**20))
TURN_LOW = float(np.float32(2 * np.pi - TURN_HIGH - TURN_MID))


def turn_reduced(angle):
    turns = jnp.floor(angle * (1.0 / (2 * np.pi)) + 0.5)
    return ((angle - turns * TURN_HIGH) - turns * TURN_MID) - turns * TURN_LOW


def split2(v):
    high = v.astype(BF16).astype(F32)
    return high, v - high


def split3(v):
    high, rest = split2(v)
    mid, low = split2(rest)
    return high, mid, low


def kernel(
    n,
    tsize,
    grid_xyc,
    width,
    lengths_s,
    from_s,
    to_v,
    table_v,
    inverse_v,
    x1_v,
    x2_v,
    gain_v,
    wq_hbm,
    wkv_hbm,
    wo_hbm,
    kc_hbm,
    vc_hbm,
    o1_v,
    o2_v,
    mk_hbm,
    mv_hbm,
    wq,
    wkv,
    wo,
    kbuf,
    vbuf,
    asm,
    send_a,
    recv_a,
    q_all,
    own_kv,
    slots_t,
    tab_v,
    tab_s,
    blocks,
    scan,
    send_c,
    recv_c,
    att_all,
    att_f,
    p_send,
    p_recv,
    kxy,
    vxy,
    sib_send,
    sib_recv,
    load_sem,
    out_sem,
    tab_sem,
    send_sem,
    recv_sem,
):
    nx, ny, nc = grid_xyc
    me = lax.axis_index("ctx")
    mt = lax.axis_index("tp")
    core = lax.rem(me, nc)
    yi = lax.rem(me // nc, ny)
    xi = me // (nc * ny)
    requests = x1_v.shape[0]
    pages = table_v.shape[1]
    slots = kbuf.shape[0]
    cap = slots - ARRIVALS
    rows_t = requests // tsize

    loads = [
        pltpu.make_async_copy(src, dst, load_sem.at[i])
        for i, (src, dst) in enumerate(
            [(wq_hbm, wq), (wkv_hbm, wkv), (kc_hbm, kbuf), (vc_hbm, vbuf), (wo_hbm, wo)]
        )
    ]
    for copy in loads:
        copy.start()

    barrier = pltpu.get_barrier_semaphore()

    def greet_ctx(j, _):
        pl.semaphore_signal(
            barrier, inc=1, device_id={"ctx": lax.rem(me + j, n)}, device_id_type=MESH
        )
        return 0

    lax.fori_loop(1, n, greet_ctx, 0)

    def greet_tp(j, _):
        pl.semaphore_signal(
            barrier, inc=1, device_id={"tp": lax.rem(mt + j, tsize)}, device_id_type=MESH
        )
        return 0

    lax.fori_loop(1, tsize, greet_tp, 0)

    def remote(src, dst, at, axis, peer):
        return pltpu.make_async_remote_copy(
            src_ref=src,
            dst_ref=dst,
            send_sem=send_sem.at[at],
            recv_sem=recv_sem.at[at],
            device_id={axis: peer},
            device_id_type=MESH,
        )

    def wait_bytes(ref, sem):
        pltpu.make_async_copy(ref, ref, sem).wait()

    x_both = jnp.concatenate([x1_v[...], x2_v[...]], axis=0).astype(F32)
    squares = jnp.sum(x_both * x_both, axis=1, keepdims=True)
    scaled = (x_both * gain_v[...].astype(F32)).astype(BF16)
    sq_high, sq_low = split2(jnp.broadcast_to(squares, (2 * requests, HEAD)))
    loads[0].wait()
    loads[1].wait()
    for step in range(2):
        rows = slice(step * requests, (step + 1) * requests)
        asm[pl.ds(20 + step, requests, stride=32), :] = sq_high[rows]
        asm[pl.ds(22 + step, requests, stride=32), :] = sq_low[rows]
    kv_part = jnp.dot(scaled, wkv[...], preferred_element_type=F32)
    for step in range(2):
        rows = slice(step * requests, (step + 1) * requests)
        asm[pl.ds(16 + step, requests, stride=32), :] = kv_part[rows, :HEAD]
        asm[pl.ds(18 + step, requests, stride=32), :] = kv_part[rows, HEAD:]
    for h in range(GROUP):
        part = jnp.dot(scaled, wq[:, h * HEAD : (h + 1) * HEAD], preferred_element_type=F32)
        for step in range(2):
            rows = slice(step * requests, (step + 1) * requests)
            asm[pl.ds(step * GROUP + h, requests, stride=32), :] = part[rows]

    pl.semaphore_wait(barrier, n - 1 + tsize - 1)

    def send_partial(j, _):
        peer = lax.rem(me + j, n)
        send_a[peer] = asm[pl.ds(pl.multiple_of(peer * 32, 32), 32), :].astype(BF16)
        remote(send_a.at[peer], recv_a.at[j], 0, "ctx", peer).start()
        return 0

    lax.fori_loop(1, n, send_partial, 0)

    loads[2].wait()
    loads[3].wait()
    for i in range(2):
        leaving = jnp.clip(from_s[2 * me + i] - me * slots, 0, slots - 1)
        kxy[yi, xi, i] = kbuf[leaving]
        vxy[xi, yi, i] = vbuf[leaving]
    for d in range(1, nx):
        peer = (lax.rem(xi + d, nx) * ny + yi) * nc + core
        remote(kxy.at[yi, xi], kxy.at[yi, xi], 5, "ctx", peer).start()
    for d in range(1, ny):
        peer = (xi * ny + lax.rem(yi + d, ny)) * nc + core
        remote(vxy.at[xi, yi], vxy.at[xi, yi], 6, "ctx", peer).start()

    local_table = table_v[...] - me * slots
    code = (
        lax.broadcasted_iota(jnp.int32, (requests, pages), 0) * pages
        + lax.broadcasted_iota(jnp.int32, (requests, pages), 1)
        + 1
    )
    slots_t[...] = jnp.zeros(slots_t.shape, jnp.int32)
    for s in range(cap):
        found = jnp.where(local_table == s, code, 0)
        slots_t[s : s + 1, :] = jnp.max(found, axis=0, keepdims=True)
    by_slot = slots_t[...]
    rows_n = tab_v.shape[0]
    code_col = jnp.max(by_slot[:rows_n], axis=1, keepdims=True)
    code_row = jnp.max(by_slot.T, axis=0, keepdims=True)
    owner_col = jnp.right_shift(code_col - 1, pages.bit_length() - 1)
    owner_row = jnp.right_shift(code_row - 1, pages.bit_length() - 1)
    wide = (rows_n, 128)
    row_id = lax.broadcasted_iota(jnp.int32, wide, 0)
    lane_id = lax.broadcasted_iota(jnp.int32, wide, 1)
    earlier = (owner_col == owner_row) & (lane_id < row_id) & (code_row > 0)
    prev_col = jnp.max(jnp.where(earlier, lane_id + 1, 0), axis=1, keepdims=True)
    held = (owner_row == row_id) & (code_row > 0)
    last_col = jnp.max(jnp.where(held, lane_id + 1, 0), axis=1, keepdims=True)
    targets = to_v[...] - cap
    moves = targets.shape[1]
    move_row = lax.broadcasted_iota(jnp.int32, (rows_n, moves), 0)
    move_lane = lax.broadcasted_iota(jnp.int32, (rows_n, moves), 1)
    sibling = me + 1 - 2 * core
    arrive_col = jnp.max(
        jnp.where(targets - me * slots == move_row, move_lane + 1, 0), axis=1, keepdims=True
    )
    arrive_sib = jnp.max(
        jnp.where(targets - sibling * slots == move_row, move_lane + 1, 0), axis=1, keepdims=True
    )
    packed = jnp.zeros(wide, jnp.int32)
    for i, column in enumerate([code_col, prev_col, last_col, arrive_col, arrive_sib]):
        packed = jnp.where(lane_id == i, column, packed)
    tab_v[...] = packed
    tab_copy = pltpu.make_async_copy(tab_v, tab_s, tab_sem)
    tab_copy.start()

    position = lengths_s[me].astype(F32)
    inverse = inverse_v[...]
    lane = lax.broadcasted_iota(jnp.int32, (1, HEAD), 1)
    sign = jnp.where(lane < HEAD // 2, -1.0, 1.0)
    angles = jnp.concatenate([position * inverse, (position + 1.0) * inverse], axis=0)
    angles = turn_reduced(angles)
    cosine = jnp.cos(angles)
    sine = jnp.sin(angles) * sign

    def by_step(v, count):
        return jnp.concatenate(
            [jnp.broadcast_to(v[0:1], (count, HEAD)), jnp.broadcast_to(v[1:2], (count, HEAD))],
            axis=0,
        )

    tab_copy.wait()
    total = asm[pl.ds(pl.multiple_of(me * 32, 32), 32), :]
    wait_bytes(recv_a.at[pl.ds(1, n - 1)], recv_sem.at[0])
    for j in range(1, n):
        total = total + recv_a[j].astype(F32)
    square = total[20:22] + total[22:24]
    rms = lax.rsqrt(square / width + EPSILON)

    def rotated(v, count):
        return v * by_step(cosine, count) + pltpu.roll(v, HEAD // 2, 1) * by_step(sine, count)

    q_own = rotated(total[:16] * by_step(rms, GROUP), GROUP).astype(BF16)
    q_all[me] = q_own

    def send_query(j, _):
        peer = lax.rem(me + j, n)
        remote(q_all.at[me], q_all.at[me], 1, "ctx", peer).start()
        return 0

    lax.fori_loop(1, n, send_query, 0)

    wait_bytes(kxy.at[0, pl.ds(0, nx - 1)], recv_sem.at[5])
    wait_bytes(vxy.at[0, pl.ds(0, ny - 1)], recv_sem.at[6])
    for d in range(1, ny):
        peer = (xi * ny + lax.rem(yi + d, ny)) * nc + core
        remote(kxy.at[yi], kxy.at[yi], 7, "ctx", peer).start()
    for d in range(1, nx):
        peer = (lax.rem(xi + d, nx) * ny + yi) * nc + core
        remote(vxy.at[xi], vxy.at[xi], 8, "ctx", peer).start()

    new_k = rotated(total[16:18] * rms, 1).astype(BF16).astype(F32)
    new_v = (total[18:20] * rms).astype(BF16).astype(F32)
    qf = q_own.astype(F32)
    second = lax.broadcasted_iota(jnp.int32, (16, HEAD), 0) >= GROUP
    own_1 = jnp.sum(qf * new_k[0:1], axis=1, keepdims=True) * SCALE
    own_2 = jnp.sum(qf * new_k[1:2], axis=1, keepdims=True) * SCALE
    own_1 = jnp.broadcast_to(own_1, (16, HEAD))
    own_2 = jnp.where(second, jnp.broadcast_to(own_2, (16, HEAD)), NEGATIVE)
    own_max = jnp.maximum(own_1, own_2)
    own_w1 = jnp.exp(own_1 - own_max).astype(BF16).astype(F32)
    own_w2 = jnp.exp(own_2 - own_max).astype(BF16).astype(F32)
    own_total = own_w1 + own_w2
    own_out = own_w1 * new_v[0:1] + own_w2 * new_v[1:2]
    own_kv[0] = own_max
    own_kv[1] = own_total
    own_kv[2] = own_out

    scan[0, 0:16] = jnp.full((16, HEAD), NEGATIVE, F32)
    scan[0, 16:48] = jnp.zeros((32, HEAD), F32)
    wait_bytes(q_all.at[pl.ds(0, n - 1)], recv_sem.at[1])
    token = lax.broadcasted_iota(jnp.int32, (16, PAGE), 1)
    per = 7 if cap % 7 == 0 else 1

    def page_block(b, _):
        for i in range(per):
            s = b * per + i
            flat = jnp.maximum(tab_s[s, 0] - 1, 0)
            present = tab_s[s, 0] > 0
            owner = jnp.right_shift(flat, pages.bit_length() - 1)
            page = jnp.bitwise_and(flat, pages - 1)
            count = jnp.where(present, lengths_s[owner] - page * PAGE, 0)
            scores = lax.dot_general(
                q_all[owner], kbuf[s], (((1,), (1,)), ((), ())), preferred_element_type=F32
            )
            valid = token < count
            scores = jnp.where(valid, scores * SCALE, NEGATIVE)
            top = jnp.max(scores, axis=1, keepdims=True)
            weights = jnp.where(valid, jnp.exp(scores - top), 0.0).astype(BF16)
            amount = jnp.sum(weights.astype(F32), axis=1, keepdims=True)
            out = jnp.dot(weights, vbuf[s], preferred_element_type=F32)
            blocks[i, 0:16] = jnp.broadcast_to(top, (16, HEAD))
            blocks[i, 16:32] = jnp.broadcast_to(amount, (16, HEAD))
            blocks[i, 32:48] = out
        for i in range(per):
            s = b * per + i
            before = tab_s[s, 1]
            top_b, top = scan[before, 0:16], blocks[i, 0:16]
            peak = jnp.maximum(top_b, top)
            scale_b, scale = jnp.exp(top_b - peak), jnp.exp(top - peak)
            scan[s + 1, 0:16] = peak
            scan[s + 1, 16:32] = scan[before, 16:32] * scale_b + blocks[i, 16:32] * scale
            scan[s + 1, 32:48] = scan[before, 32:48] * scale_b + blocks[i, 32:48] * scale
        return 0

    lax.fori_loop(0, cap // per, page_block, 0)

    lane16 = lax.broadcasted_iota(jnp.int32, (16, HEAD), 1)

    def message(r):
        at = tab_s[r, 2]
        t3 = split3(scan[at, 0:16])
        a2 = split2(scan[at, 16:32])
        small = jnp.zeros((16, HEAD), F32)
        for i, part in enumerate(t3 + a2):
            small = jnp.where(lane16 == i, part, small)
        return scan[at, 32:48].astype(BF16), small.astype(BF16)

    def send_blocks(j, _):
        peer = lax.rem(me + j, n)
        big, small = message(peer)
        send_c[peer, 0:16] = big
        send_c[peer, 16:32] = small
        remote(send_c.at[peer], recv_c.at[j], 2, "ctx", peer).start()
        return 0

    lax.fori_loop(1, n, send_blocks, 0)
    big, small = message(me)
    recv_c[0, 0:16] = big
    recv_c[0, 16:32] = small

    leave_0 = from_s[2 * me] - me * slots
    leave_1 = from_s[2 * me + 1] - me * slots

    def clear(s, _):
        gone = (s == leave_0) | (s == leave_1)
        kbuf[s] = jnp.where(gone, jnp.zeros((), BF16), kbuf[s])
        vbuf[s] = jnp.where(gone, jnp.zeros((), BF16), vbuf[s])
        return 0

    lax.fori_loop(0, cap, clear, 0)

    pick = lax.broadcasted_iota(jnp.int32, (HEAD, 2 * HEAD), 0)
    half = lax.broadcasted_iota(jnp.int32, (HEAD, 2 * HEAD), 1) >= HEAD
    chooser = jnp.where(
        half, jnp.where((pick == 3) | (pick == 4), 1.0, 0.0), jnp.where(pick < 3, 1.0, 0.0)
    ).astype(BF16)
    wait_bytes(recv_c.at[pl.ds(1, n - 1)], recv_sem.at[2])
    spread = jnp.dot(
        recv_c[:, 16:32].reshape(n * 16, HEAD), chooser, preferred_element_type=F32
    )
    for j in range(n):
        asm[j * 32 : j * 32 + 16, :] = spread[j * 16 : j * 16 + 16, :HEAD]
        asm[j * 32 + 16 : j * 32 + 32, :] = spread[j * 16 : j * 16 + 16, HEAD:]
    peak = own_kv[0]
    for j in range(n):
        peak = jnp.maximum(peak, asm[j * 32 : j * 32 + 16, :])
    own_scale = jnp.exp(own_kv[0] - peak)
    denominator = own_kv[1] * own_scale
    numerator = own_kv[2] * own_scale
    for j in range(n):
        scale = jnp.exp(asm[j * 32 : j * 32 + 16, :] - peak)
        denominator = denominator + asm[j * 32 + 16 : j * 32 + 32, :] * scale
        numerator = numerator + recv_c[j, 0:16].astype(F32) * scale
    att_all[me] = (numerator / denominator).astype(BF16)

    def send_attention(j, _):
        peer = lax.rem(me + j, n)
        remote(att_all.at[me], att_all.at[me], 3, "ctx", peer).start()
        return 0

    lax.fori_loop(1, n, send_attention, 0)

    wait_bytes(kxy.at[pl.ds(0, ny - 1)], recv_sem.at[7])
    wait_bytes(vxy.at[pl.ds(0, nx - 1)], recv_sem.at[8])

    def source_of(mark):
        index = jnp.maximum(mark - 1, 0)
        device = jnp.right_shift(index, 1)
        which = jnp.bitwise_and(index, 1)
        src_core = lax.rem(device, nc)
        src_y = lax.rem(device // nc, ny)
        src_x = device // (nc * ny)
        return src_x, src_y, src_core, which

    for i in range(ARRIVALS):
        src_x, src_y, _, which = source_of(tab_s[i, 4])
        sib_send[0, i] = kxy[src_y, src_x, which]
        sib_send[1, i] = vxy[src_x, src_y, which]
    remote(sib_send, sib_recv, 9, "ctx", sibling).start()

    loads[4].wait()
    wait_bytes(att_all.at[pl.ds(0, n - 1)], recv_sem.at[3])
    for r in range(requests):
        att_f[r * 16 : r * 16 + 16, :] = att_all[r].astype(F32)
    attention = jnp.concatenate(
        [
            jnp.concatenate(
                [att_f[pl.ds(step * GROUP + h, requests, stride=16), :] for h in range(GROUP)],
                axis=1,
            )
            for step in range(2)
        ],
        axis=0,
    ).astype(BF16)
    projected = jnp.dot(attention, wo[...], preferred_element_type=F32)
    for t in range(tsize):
        for step in range(2):
            p_send[t, step * rows_t : (step + 1) * rows_t] = projected[
                step * requests + t * rows_t : step * requests + (t + 1) * rows_t
            ]

    def send_projected(j, _):
        peer = lax.rem(mt + j, tsize)
        remote(p_send.at[peer], p_recv.at[j], 4, "tp", peer).start()
        return 0

    lax.fori_loop(1, tsize, send_projected, 0)

    wait_bytes(sib_recv, recv_sem.at[9])
    for i in range(ARRIVALS):
        mark = tab_s[i, 3]
        src_x, src_y, src_core, which = source_of(mark)
        here = src_core == core
        arrived = mark > 0
        new_page = jnp.where(here, kxy[src_y, src_x, which], sib_recv[0, i])
        kbuf[cap + i] = jnp.where(arrived, new_page, kbuf[cap + i])
        new_page = jnp.where(here, vxy[src_x, src_y, which], sib_recv[1, i])
        vbuf[cap + i] = jnp.where(arrived, new_page, vbuf[cap + i])
    out_k = pltpu.make_async_copy(kbuf, mk_hbm, out_sem.at[0])
    out_v = pltpu.make_async_copy(vbuf, mv_hbm, out_sem.at[1])
    out_k.start()
    out_v.start()

    residual_1 = jnp.zeros((rows_t, x1_v.shape[1]), F32)
    residual_2 = residual_1
    x1_f, x2_f = x1_v[...].astype(F32), x2_v[...].astype(F32)
    for t in range(tsize):
        rows = slice(t * rows_t, (t + 1) * rows_t)
        residual_1 = jnp.where(mt == t, x1_f[rows], residual_1)
        residual_2 = jnp.where(mt == t, x2_f[rows], residual_2)

    wait_bytes(p_recv.at[pl.ds(1, tsize - 1)], recv_sem.at[4])
    summed = p_send[mt]
    for j in range(1, tsize):
        summed = summed + p_recv[j]
    o1_v[...] = (residual_1 + summed[:rows_t]).astype(BF16)
    o2_v[...] = (residual_2 + summed[rows_t:]).astype(BF16)

    wait_bytes(recv_a.at[pl.ds(1, n - 1)], send_sem.at[0])
    wait_bytes(q_all.at[pl.ds(0, n - 1)], send_sem.at[1])
    wait_bytes(recv_c.at[pl.ds(1, n - 1)], send_sem.at[2])
    wait_bytes(att_all.at[pl.ds(0, n - 1)], send_sem.at[3])
    wait_bytes(p_recv.at[pl.ds(1, tsize - 1)], send_sem.at[4])
    wait_bytes(kxy.at[0, pl.ds(0, nx - 1)], send_sem.at[5])
    wait_bytes(vxy.at[0, pl.ds(0, ny - 1)], send_sem.at[6])
    wait_bytes(kxy.at[pl.ds(0, ny - 1)], send_sem.at[7])
    wait_bytes(vxy.at[pl.ds(0, nx - 1)], send_sem.at[8])
    wait_bytes(sib_send, send_sem.at[9])
    out_k.wait()
    out_v.wait()


def grid_of(n):
    cores = 2
    side = int(round((n // cores) ** 0.5))
    return (n // cores // side, side, cores)


def per_device(
    n,
    tsize,
    x_first,
    x_second,
    norm_gain,
    w_query,
    key_value_weight,
    w_out,
    key_cache,
    value_cache,
    lengths,
    page_table,
    move_from,
    move_to,
):
    requests, depth = x_first.shape
    slots = key_cache.shape[0]
    cap = slots - ARRIVALS
    nx, ny, nc = grid_of(n)
    rows_t = requests // tsize
    half = HEAD // 2
    inverse = THETA ** (-(np.arange(half, dtype=np.float64) * 2.0 / HEAD))
    inverse = np.concatenate([inverse, inverse])[None, :].astype(np.float32)
    rows_n = -(-max(cap, requests) // 8) * 8
    vmem = pl.BlockSpec(memory_space=pltpu.VMEM)
    smem = pl.BlockSpec(memory_space=pltpu.SMEM)
    anywhere = pl.BlockSpec(memory_space=pl.ANY)
    out = pl.pallas_call(
        functools.partial(kernel, n, tsize, (nx, ny, nc), depth * n),
        out_shape=(
            jax.ShapeDtypeStruct((rows_t, depth), BF16),
            jax.ShapeDtypeStruct((rows_t, depth), BF16),
            jax.ShapeDtypeStruct(key_cache.shape, BF16),
            jax.ShapeDtypeStruct(value_cache.shape, BF16),
        ),
        in_specs=[smem, smem] + [vmem] * 6 + [anywhere] * 5,
        out_specs=(vmem, vmem, anywhere, anywhere),
        scratch_shapes=[
            pltpu.VMEM(w_query.shape, BF16),
            pltpu.VMEM(key_value_weight.shape, BF16),
            pltpu.VMEM(w_out.shape, BF16),
            pltpu.VMEM(key_cache.shape, BF16),
            pltpu.VMEM(value_cache.shape, BF16),
            pltpu.VMEM((n * 32, HEAD), F32),
            pltpu.VMEM((n, 32, HEAD), BF16),
            pltpu.VMEM((n, 32, HEAD), BF16),
            pltpu.VMEM((n, 16, HEAD), BF16),
            pltpu.VMEM((3, 16, HEAD), F32),
            pltpu.VMEM((128, page_table.shape[1]), jnp.int32),
            pltpu.VMEM((rows_n, 128), jnp.int32),
            pltpu.SMEM((rows_n, 128), jnp.int32),
            pltpu.VMEM((8, 48, HEAD), F32),
            pltpu.VMEM((cap + 1, 48, HEAD), F32),
            pltpu.VMEM((n, 32, HEAD), BF16),
            pltpu.VMEM((n, 32, HEAD), BF16),
            pltpu.VMEM((n, 16, HEAD), BF16),
            pltpu.VMEM((n * 16, HEAD), F32),
            pltpu.VMEM((tsize, 2 * rows_t, depth), F32),
            pltpu.VMEM((tsize, 2 * rows_t, depth), F32),
            pltpu.VMEM((ny, nx, 2, PAGE, HEAD), BF16),
            pltpu.VMEM((nx, ny, 2, PAGE, HEAD), BF16),
            pltpu.VMEM((2, ARRIVALS, PAGE, HEAD), BF16),
            pltpu.VMEM((2, ARRIVALS, PAGE, HEAD), BF16),
            pltpu.SemaphoreType.DMA((5,)),
            pltpu.SemaphoreType.DMA((2,)),
            pltpu.SemaphoreType.DMA,
            pltpu.SemaphoreType.DMA((10,)),
            pltpu.SemaphoreType.DMA((10,)),
        ],
        compiler_params=pltpu.CompilerParams(
            collective_id=0, has_side_effects=True, vmem_limit_bytes=40 * 1024 * 1024
        ),
        name="decode_two_steps",
    )(
        lengths,
        move_from,
        move_to.reshape(1, -1),
        page_table,
        jnp.asarray(inverse),
        x_first,
        x_second,
        norm_gain.reshape(1, -1),
        w_query,
        key_value_weight,
        w_out,
        key_cache,
        value_cache,
    )
    return out


def solution(mesh):
    n, tsize = mesh.shape["ctx"], mesh.shape["tp"]
    in_specs = (
        P(None, "ctx"),
        P(None, "ctx"),
        P("ctx"),
        P("ctx", "tp"),
        P("ctx", "tp"),
        P("tp", "ctx"),
        P("ctx", None, "tp"),
        P("ctx", None, "tp"),
        P(),
        P(),
        P(),
        P(),
    )
    out_specs = (P("tp", "ctx"), P("tp", "ctx"), P("ctx", None, "tp"), P("ctx", None, "tp"))
    return jax.shard_map(
        functools.partial(per_device, n, tsize),
        mesh=mesh,
        in_specs=in_specs,
        out_specs=out_specs,
        check_vma=False,
    )
```

time: 607 us -> 69.3 us (0.11); the launches traced: 598 us -> 68.8 us
  waiting for transfers between devices: 286 us -> 0 us
  blocking collectives: 108 us -> 0 us
  other arithmetic: 74.2 us -> 0 us
  local copies, waits for them, and re-layouts: 85.2 us -> 14.4 us
  Pallas kernels: 0 us -> 53.7 us
  matrix products: 25 us -> 0 us
  between operations: 16.4 us -> 0.65 us
    psum x2 -> x0, waiting for transfers between devices: 212 us -> none  [project_local(): lax.psum((squares, query_portion, keyval_part), 'ctx')]
    all_gather x4 -> x0, blocking collectives: 95.5 us -> none  [combined_all(): everything = jax.tree.map(lambda part: lax.all_gather(part, axis), x)]
    unnamed x8 -> x0, waiting for transfers between devices: 64.4 us -> none
    dynamic_slice x62 -> x0, local copies, waits for them, and re-layouts: 57.4 us -> none  [lap(): return combine(so_far, jax.tree.map(lambda part: part[k], everything))]
    pallas_call x0 -> x1, Pallas kernels: none -> 53.7 us  [per_device(): pl.pallas_call(functools.partial(kernel, n, tsize, (nx, ny, nc), depth *...]
    mul x127 -> x0, other arithmetic: 44.9 us -> none  [the longest x62 22.2 us: combine_parts(): later[2] * second_scale[..., None]]
    dot_general x19 -> x0, matrix products: 25 us -> none  [the longest x1 4.29 us: per_device(): jnp.einsum('sn,npw->spw', placing_matrix, piece_v, preferred_element_type...]
    unnamed x1 -> x0, blocking collectives: 13 us -> none
  transfers between devices with their start and end apart: 7 -> 0, of which waited for: 5 -> 0; matrix products, arithmetic and copies ran while one was open for 22% -> 0% of each run, Pallas kernels for 0% -> 0%
where the time goes in v1:
time: 69.3 us; the launch traced here: 68.8 us
  Pallas kernels  53.7 us (77%)
  local copies, waits for them, and re-layouts  14.4 us (21%)
    pallas_call x1, Pallas kernels, per_device(): pl.pallas_call(functools.partial(kernel, n, tsize, (nx, ny, nc), depth *...  53.7 us
    unnamed x28, local copies, waits for them, and re-layouts  13.8 us

profile of v1, /device:TPU:1, one launch (start us, length us, event | category | flops | bytes accessed | tf_op | source)
XLA Modules:
  0.0 68.8 jit_solution(13486906713357849309)
XLA Ops:
  0.6 0.7 reshape.15.gain_v
  1.3 0.0 copy-start
  1.3 1.3 %copy-done = bf16[43,128,128]{2,1,0:T(8,128)(2,1)S(1)} copy-done((bf16[43,128,128]{2,1,0:T(8,128)(2,1)S(1)}, bf16[43,128,128]{2,1,0:T(8,128)(2,1)}, u32[]{:S(2)}) %copy-start) | copy-done | bytes 1409048
  2.6 0.0 copy-start.1
  2.6 1.3 %copy-done.1 = bf16[43,128,128]{2,1,0:T(8,128)(2,1)S(1)} copy-done((bf16[43,128,128]{2,1,0:T(8,128)(2,1)S(1)}, bf16[43,128,128]{2,1,0:T(8,128)(2,1)}, u32[]{:S(2)}) %copy-start.1) | copy-done | bytes 1409048
  4.0 0.0 copy-start.2
  4.0 1.0 %copy-done.2 = bf16[256,1024]{1,0:T(8,128)(2,1)S(1)} copy-done((bf16[256,1024]{1,0:T(8,128)(2,1)S(1)}, bf16[256,1024]{1,0:T(8,128)(2,1)}, u32[]{:S(2)}) %copy-start.2) | copy-done | bytes 524312
  5.0 0.0 copy-start.3
  5.0 1.0 %copy-done.3 = bf16[1024,256]{1,0:T(8,128)(2,1)S(1)} copy-done((bf16[1024,256]{1,0:T(8,128)(2,1)S(1)}, bf16[1024,256]{1,0:T(8,128)(2,1)}, u32[]{:S(2)}) %copy-start.3) | copy-done | bytes 524312
  6.1 0.0 copy-start.4
  6.1 0.9 %copy-done.4 = bf16[256,256]{1,0:T(8,128)(2,1)S(1)} copy-done((bf16[256,256]{1,0:T(8,128)(2,1)S(1)}, bf16[256,256]{1,0:T(8,128)(2,1)}, u32[]{:S(2)}) %copy-start.4) | copy-done | bytes 131096
  7.0 0.0 copy-start.5
  7.0 0.7 %copy-done.5 = s32[32,128]{1,0:T(8,128)S(1)} copy-done((s32[32,128]{1,0:T(8,128)S(1)}, s32[32,128]{1,0:T(8,128)}, u32[]{:S(2)}) %copy-start.5) | copy-done | bytes 16408
  7.7 0.7 %copy-done.6 = bf16[32,256]{1,0:T(8,128)(2,1)S(1)} copy-done((bf16[32,256]{1,0:T(8,128)(2,1)S(1)}, bf16[32,256]{1,0:T(8,128)(2,1)}, u32[]{:S(2)}) %copy-start.6) | copy-done | bytes 16408
  8.4 0.7 %copy-done.7 = bf16[32,256]{1,0:T(8,128)(2,1)S(1)} copy-done((bf16[32,256]{1,0:T(8,128)(2,1)S(1)}, bf16[32,256]{1,0:T(8,128)(2,1)}, u32[]{:S(2)}) %copy-start.7) | copy-done | bytes 16408
  9.1 0.7 copy-done.8
  9.8 0.7 copy-done.9
  10.4 0.7 copy-done.10
  11.1 0.7 copy-done.11
  11.8 53.7 %decode_two_steps.1 = (bf16[4,256]{1,0:T(4,128)(2,1)S(1)}, bf16[4,256]{1,0:T(4,128)(2,1)S(1)}, bf16[43,128,128]{2,1,0:T(8,128)(2,1)S(1)}, bf16[43,128,128]{2,1,0:T(8,128)(2,1)S(1)}) custom-call(s32[32]{0:T(128)S(1)} %copy-done.8, s32[64]{0:T(128)S(1)} %copy-done.9, s32[1,64]{1,0:T(1,128)S(1)} %bitcast.1, s32[32,128]{1,0:T(8,128)S(1)} %copy-done.5, ...), custom_call_target="tpu_custom_call" | custom-call | tf_op jit(solution)/shard_map/decode_two_steps/pallas_call | solution.py:525
  65.5 0.6 copy.21
  66.0 0.6 copy.22
  66.6 1.1 %copy.23 = bf16[43,128,128]{2,1,0:T(8,128)(2,1)} copy(bf16[43,128,128]{2,1,0:T(8,128)(2,1)S(1)} %get-tuple-element.10) | data formatting | bytes 2818048
  67.7 1.1 %copy.24 = bf16[43,128,128]{2,1,0:T(8,128)(2,1)} copy(bf16[43,128,128]{2,1,0:T(8,128)(2,1)S(1)} %get-tuple-element.11) | data formatting | bytes 2818048
  (6 shorter events, 0.0 us)
Async XLA Ops:
  1.3 1.4 %copy-start = (bf16[43,128,128]{2,1,0:T(8,128)(2,1)S(1)}, bf16[43,128,128]{2,1,0:T(8,128)(2,1)}, u32[]{:S(2)}) copy-start(bf16[43,128,128]{2,1,0:T(8,128)(2,1)} %kc_hbm.1) | copy-start | bytes 4227076
  2.6 1.4 %copy-start.1 = (bf16[43,128,128]{2,1,0:T(8,128)(2,1)S(1)}, bf16[43,128,128]{2,1,0:T(8,128)(2,1)}, u32[]{:S(2)}) copy-start(bf16[43,128,128]{2,1,0:T(8,128)(2,1)} %vc_hbm.1) | copy-start | bytes 4227076
  4.0 1.0 %copy-start.2 = (bf16[256,1024]{1,0:T(8,128)(2,1)S(1)}, bf16[256,1024]{1,0:T(8,128)(2,1)}, u32[]{:S(2)}) copy-start(bf16[256,1024]{1,0:T(8,128)(2,1)} %wq_hbm.1) | copy-start | bytes 1572868
  5.0 1.0 %copy-start.3 = (bf16[1024,256]{1,0:T(8,128)(2,1)S(1)}, bf16[1024,256]{1,0:T(8,128)(2,1)}, u32[]{:S(2)}) copy-start(bf16[1024,256]{1,0:T(8,128)(2,1)} %wo_hbm.1) | copy-start | bytes 1572868
  6.1 0.9 %copy-start.4 = (bf16[256,256]{1,0:T(8,128)(2,1)S(1)}, bf16[256,256]{1,0:T(8,128)(2,1)}, u32[]{:S(2)}) copy-start(bf16[256,256]{1,0:T(8,128)(2,1)} %wkv_hbm.1) | copy-start | bytes 393220
  7.0 0.7 %copy-start.5 = (s32[32,128]{1,0:T(8,128)S(1)}, s32[32,128]{1,0:T(8,128)}, u32[]{:S(2)}) copy-start(s32[32,128]{1,0:T(8,128)} %table_v.1) | copy-start | bytes 49156
  7.7 0.7 %copy-start.6 = (bf16[32,256]{1,0:T(8,128)(2,1)S(1)}, bf16[32,256]{1,0:T(8,128)(2,1)}, u32[]{:S(2)}) copy-start(bf16[32,256]{1,0:T(8,128)(2,1)} %x1_v.1) | copy-start | bytes 49156
  8.4 0.7 %copy-start.7 = (bf16[32,256]{1,0:T(8,128)(2,1)S(1)}, bf16[32,256]{1,0:T(8,128)(2,1)}, u32[]{:S(2)}) copy-start(bf16[32,256]{1,0:T(8,128)(2,1)} %x2_v.1) | copy-start | bytes 49156
  9.1 0.7 copy-start.8
  9.8 0.7 copy-start.9
  10.4 0.7 copy-start.10
  11.1 0.7 copy-start.11

commit v2 on v1

--- a/solution.py
+++ b/solution.py
@@ -19,6 +19,9 @@
 MESH = pl.DeviceIdType.MESH
 F32 = jnp.float32
 BF16 = jnp.bfloat16
+VMEM_GRANT = 58 * 1024 * 1024
+AFTER_QUERY, AFTER_BLOCKS = 2, 1
+CHUNKS = 4
 
 TURN_HIGH = 6.28125
 TURN_MID = float(np.float32(np.round((2 * np.pi - TURN_HIGH) * 2.0**20) / 2.0**20))
@@ -33,12 +36,6 @@
 def split2(v):
     high = v.astype(BF16).astype(F32)
     return high, v - high
-
-
-def split3(v):
-    high, rest = split2(v)
-    mid, low = split2(rest)
-    return high, mid, low
 
 
 def kernel(
@@ -46,14 +43,13 @@
     tsize,
     grid_xyc,
     width,
-    lengths_s,
-    from_s,
-    to_v,
-    table_v,
-    inverse_v,
-    x1_v,
-    x2_v,
-    gain_v,
+    lengths_hbm,
+    from_hbm,
+    to_hbm,
+    table_hbm,
+    x1_hbm,
+    x2_hbm,
+    gain_hbm,
     wq_hbm,
     wkv_hbm,
     wo_hbm,
@@ -63,6 +59,13 @@
     o2_v,
     mk_hbm,
     mv_hbm,
+    lengths_s,
+    from_s,
+    to_v,
+    table_v,
+    x1_v,
+    x2_v,
+    gain_v,
     wq,
     wkv,
     wo,
@@ -76,10 +79,14 @@
     slots_t,
     tab_v,
     tab_s,
+    scores,
+    weights,
     blocks,
     scan,
     send_c,
     recv_c,
+    send_m,
+    recv_m,
     att_all,
     att_f,
     p_send,
@@ -109,29 +116,49 @@
     loads = [
         pltpu.make_async_copy(src, dst, load_sem.at[i])
         for i, (src, dst) in enumerate(
-            [(wq_hbm, wq), (wkv_hbm, wkv), (kc_hbm, kbuf), (vc_hbm, vbuf), (wo_hbm, wo)]
+            [
+                (wq_hbm, wq),
+                (wkv_hbm, wkv),
+                (kc_hbm, kbuf),
+                (vc_hbm, vbuf),
+                (wo_hbm, wo),
+                (x1_hbm, x1_v),
+                (x2_hbm, x2_v),
+                (gain_hbm, gain_v),
+                (lengths_hbm, lengths_s),
+                (from_hbm, from_s),
+                (to_hbm, to_v.at[0]),
+                (table_hbm, table_v),
+            ]
         )
     ]
-    for copy in loads:
-        copy.start()
+    for at in (5, 6, 7, 1, 0, 2, 3, 8, 9, 10, 11, 4):
+        loads[at].start()
+
+    def hops(d, size):
+        return min(d, size - d)
+
+    offsets = [(a, b, c) for a in range(nx) for b in range(ny) for c in range(nc)][1:]
+    offsets.sort(key=lambda o: -(hops(o[0], nx) + hops(o[1], ny)))
+    peers = [
+        (
+            (lax.rem(xi + a, nx) * ny + lax.rem(yi + b, ny)) * nc + lax.rem(core + c, nc),
+            (a * ny + b) * nc + c,
+        )
+        for a, b, c in offsets
+    ]
+
+    def far_first(size):
+        return sorted(range(1, size), key=lambda d: -hops(d, size))
 
     barrier = pltpu.get_barrier_semaphore()
 
-    def greet_ctx(j, _):
-        pl.semaphore_signal(
-            barrier, inc=1, device_id={"ctx": lax.rem(me + j, n)}, device_id_type=MESH
-        )
-        return 0
-
-    lax.fori_loop(1, n, greet_ctx, 0)
-
-    def greet_tp(j, _):
+    for peer, _ in peers:
+        pl.semaphore_signal(barrier, inc=1, device_id={"ctx": peer}, device_id_type=MESH)
+    for j in far_first(tsize):
         pl.semaphore_signal(
             barrier, inc=1, device_id={"tp": lax.rem(mt + j, tsize)}, device_id_type=MESH
         )
-        return 0
-
-    lax.fori_loop(1, tsize, greet_tp, 0)
 
     def remote(src, dst, at, axis, peer):
         return pltpu.make_async_remote_copy(
@@ -146,9 +173,11 @@
     def wait_bytes(ref, sem):
         pltpu.make_async_copy(ref, ref, sem).wait()
 
+    for at in (5, 6, 7):
+        loads[at].wait()
     x_both = jnp.concatenate([x1_v[...], x2_v[...]], axis=0).astype(F32)
     squares = jnp.sum(x_both * x_both, axis=1, keepdims=True)
-    scaled = (x_both * gain_v[...].astype(F32)).astype(BF16)
+    scaled = (x_both * gain_v[...].astype(F32)[None, :]).astype(BF16)
     sq_high, sq_low = split2(jnp.broadcast_to(squares, (2 * requests, HEAD)))
     loads[0].wait()
     loads[1].wait()
@@ -167,26 +196,23 @@
             rows = slice(step * requests, (step + 1) * requests)
             asm[pl.ds(step * GROUP + h, requests, stride=32), :] = part[rows]
 
+    for r in range(requests):
+        send_a[r] = asm[r * 32 : r * 32 + 32, :].astype(BF16)
     pl.semaphore_wait(barrier, n - 1 + tsize - 1)
 
-    def send_partial(j, _):
-        peer = lax.rem(me + j, n)
-        send_a[peer] = asm[pl.ds(pl.multiple_of(peer * 32, 32), 32), :].astype(BF16)
-        remote(send_a.at[peer], recv_a.at[j], 0, "ctx", peer).start()
-        return 0
-
-    lax.fori_loop(1, n, send_partial, 0)
-
-    loads[2].wait()
-    loads[3].wait()
+    for peer, at in peers:
+        remote(send_a.at[peer], recv_a.at[at], 0, "ctx", peer).start()
+
+    for at in (2, 3, 8, 9, 10, 11):
+        loads[at].wait()
     for i in range(2):
         leaving = jnp.clip(from_s[2 * me + i] - me * slots, 0, slots - 1)
         kxy[yi, xi, i] = kbuf[leaving]
         vxy[xi, yi, i] = vbuf[leaving]
-    for d in range(1, nx):
+    for d in far_first(nx):
         peer = (lax.rem(xi + d, nx) * ny + yi) * nc + core
         remote(kxy.at[yi, xi], kxy.at[yi, xi], 5, "ctx", peer).start()
-    for d in range(1, ny):
+    for d in far_first(ny):
         peer = (xi * ny + lax.rem(yi + d, ny)) * nc + core
         remote(vxy.at[xi, yi], vxy.at[xi, yi], 6, "ctx", peer).start()
 
@@ -232,8 +258,11 @@
     tab_copy.start()
 
     position = lengths_s[me].astype(F32)
-    inverse = inverse_v[...]
     lane = lax.broadcasted_iota(jnp.int32, (1, HEAD), 1)
+    inverse = jnp.zeros((1, HEAD), F32)
+    for i in range(HEAD // 2):
+        rate = float(np.float32(THETA ** (-2.0 * i / HEAD)))
+        inverse = jnp.where(lane % (HEAD // 2) == i, rate, inverse)
     sign = jnp.where(lane < HEAD // 2, -1.0, 1.0)
     angles = jnp.concatenate([position * inverse, (position + 1.0) * inverse], axis=0)
     angles = turn_reduced(angles)
@@ -260,21 +289,23 @@
     q_own = rotated(total[:16] * by_step(rms, GROUP), GROUP).astype(BF16)
     q_all[me] = q_own
 
-    def send_query(j, _):
-        peer = lax.rem(me + j, n)
+    for peer, _ in peers:
         remote(q_all.at[me], q_all.at[me], 1, "ctx", peer).start()
-        return 0
-
-    lax.fori_loop(1, n, send_query, 0)
 
     wait_bytes(kxy.at[0, pl.ds(0, nx - 1)], recv_sem.at[5])
     wait_bytes(vxy.at[0, pl.ds(0, ny - 1)], recv_sem.at[6])
-    for d in range(1, ny):
-        peer = (xi * ny + lax.rem(yi + d, ny)) * nc + core
-        remote(kxy.at[yi], kxy.at[yi], 7, "ctx", peer).start()
-    for d in range(1, nx):
-        peer = (lax.rem(xi + d, nx) * ny + yi) * nc + core
-        remote(vxy.at[xi], vxy.at[xi], 8, "ctx", peer).start()
+
+    def second_hop(first, last):
+        for part in range(first, min(last, nx)):
+            for d in far_first(ny):
+                peer = (xi * ny + lax.rem(yi + d, ny)) * nc + core
+                remote(kxy.at[yi, part], kxy.at[yi, part], 7, "ctx", peer).start()
+        for part in range(first, min(last, ny)):
+            for d in far_first(nx):
+                peer = (lax.rem(xi + d, nx) * ny + yi) * nc + core
+                remote(vxy.at[xi, part], vxy.at[xi, part], 8, "ctx", peer).start()
+
+    second_hop(0, AFTER_QUERY)
 
     new_k = rotated(total[16:18] * rms, 1).astype(BF16).astype(F32)
     new_v = (total[18:20] * rms).astype(BF16).astype(F32)
@@ -297,90 +328,77 @@
     scan[0, 16:48] = jnp.zeros((32, HEAD), F32)
     wait_bytes(q_all.at[pl.ds(0, n - 1)], recv_sem.at[1])
     token = lax.broadcasted_iota(jnp.int32, (16, PAGE), 1)
-    per = 7 if cap % 7 == 0 else 1
-
-    def page_block(b, _):
-        for i in range(per):
-            s = b * per + i
-            flat = jnp.maximum(tab_s[s, 0] - 1, 0)
-            present = tab_s[s, 0] > 0
-            owner = jnp.right_shift(flat, pages.bit_length() - 1)
-            page = jnp.bitwise_and(flat, pages - 1)
-            count = jnp.where(present, lengths_s[owner] - page * PAGE, 0)
-            scores = lax.dot_general(
-                q_all[owner], kbuf[s], (((1,), (1,)), ((), ())), preferred_element_type=F32
-            )
-            valid = token < count
-            scores = jnp.where(valid, scores * SCALE, NEGATIVE)
-            top = jnp.max(scores, axis=1, keepdims=True)
-            weights = jnp.where(valid, jnp.exp(scores - top), 0.0).astype(BF16)
-            amount = jnp.sum(weights.astype(F32), axis=1, keepdims=True)
-            out = jnp.dot(weights, vbuf[s], preferred_element_type=F32)
-            blocks[i, 0:16] = jnp.broadcast_to(top, (16, HEAD))
-            blocks[i, 16:32] = jnp.broadcast_to(amount, (16, HEAD))
-            blocks[i, 32:48] = out
-        for i in range(per):
-            s = b * per + i
-            before = tab_s[s, 1]
-            top_b, top = scan[before, 0:16], blocks[i, 0:16]
-            peak = jnp.maximum(top_b, top)
-            scale_b, scale = jnp.exp(top_b - peak), jnp.exp(top - peak)
-            scan[s + 1, 0:16] = peak
-            scan[s + 1, 16:32] = scan[before, 16:32] * scale_b + blocks[i, 16:32] * scale
-            scan[s + 1, 32:48] = scan[before, 32:48] * scale_b + blocks[i, 32:48] * scale
-        return 0
-
-    lax.fori_loop(0, cap // per, page_block, 0)
+    for s in range(cap):
+        flat = jnp.maximum(tab_s[s, 0] - 1, 0)
+        present = tab_s[s, 0] > 0
+        owner = jnp.right_shift(flat, pages.bit_length() - 1)
+        page = jnp.bitwise_and(flat, pages - 1)
+        count = jnp.where(present, lengths_s[owner] - page * PAGE, 0)
+        product = lax.dot_general(
+            q_all[owner], kbuf[s], (((1,), (1,)), ((), ())), preferred_element_type=F32
+        )
+        scores[s] = jnp.where(token < count, product * SCALE, NEGATIVE)
+    for s in range(cap):
+        flat = jnp.maximum(tab_s[s, 0] - 1, 0)
+        present = tab_s[s, 0] > 0
+        owner = jnp.right_shift(flat, pages.bit_length() - 1)
+        page = jnp.bitwise_and(flat, pages - 1)
+        count = jnp.where(present, lengths_s[owner] - page * PAGE, 0)
+        row = scores[s]
+        top = jnp.max(row, axis=1, keepdims=True)
+        exact = jnp.where(token < count, jnp.exp(row - top), 0.0).astype(BF16)
+        weights[s] = exact
+        blocks[s, 0:16] = jnp.broadcast_to(top, (16, HEAD))
+        blocks[s, 16:32] = jnp.broadcast_to(
+            jnp.sum(exact.astype(F32), axis=1, keepdims=True), (16, HEAD)
+        )
+    for s in range(cap):
+        blocks[s, 32:48] = jnp.dot(weights[s], vbuf[s], preferred_element_type=F32)
+    for s in range(cap):
+        before = tab_s[s, 1]
+        top_b, top = scan[before, 0:16], blocks[s, 0:16]
+        peak = jnp.maximum(top_b, top)
+        scale_b, scale = jnp.exp(top_b - peak), jnp.exp(top - peak)
+        scan[s + 1, 0:16] = peak
+        scan[s + 1, 16:32] = scan[before, 16:32] * scale_b + blocks[s, 16:32] * scale
+        scan[s + 1, 32:48] = scan[before, 32:48] * scale_b + blocks[s, 32:48] * scale
 
     lane16 = lax.broadcasted_iota(jnp.int32, (16, HEAD), 1)
-
-    def message(r):
+    row16 = lax.broadcasted_iota(jnp.int32, (16, HEAD), 0)
+    for r in range(requests):
         at = tab_s[r, 2]
-        t3 = split3(scan[at, 0:16])
-        a2 = split2(scan[at, 16:32])
-        small = jnp.zeros((16, HEAD), F32)
-        for i, part in enumerate(t3 + a2):
-            small = jnp.where(lane16 == i, part, small)
-        return scan[at, 32:48].astype(BF16), small.astype(BF16)
-
-    def send_blocks(j, _):
-        peer = lax.rem(me + j, n)
-        big, small = message(peer)
-        send_c[peer, 0:16] = big
-        send_c[peer, 16:32] = small
-        remote(send_c.at[peer], recv_c.at[j], 2, "ctx", peer).start()
-        return 0
-
-    lax.fori_loop(1, n, send_blocks, 0)
-    big, small = message(me)
-    recv_c[0, 0:16] = big
-    recv_c[0, 16:32] = small
+        send_c[r] = scan[at, 32:48].astype(BF16)
+        both = jnp.where(lane16 == row16 + 16, scan[at, 16:32], 0.0)
+        both = jnp.where(lane16 == row16, scan[at, 0:16], both)
+        send_m[r] = jnp.sum(both, axis=0, keepdims=True)
+    for peer, at in peers:
+        remote(send_m.at[peer], recv_m.at[at], 10, "ctx", peer).start()
+        remote(send_c.at[peer], recv_c.at[at], 2, "ctx", peer).start()
+    recv_c[0] = send_c[me]
+    recv_m[0] = send_m[me]
+    second_hop(AFTER_QUERY, AFTER_QUERY + AFTER_BLOCKS)
 
     leave_0 = from_s[2 * me] - me * slots
     leave_1 = from_s[2 * me + 1] - me * slots
 
-    def clear(s, _):
+    for s in range(cap):
         gone = (s == leave_0) | (s == leave_1)
         kbuf[s] = jnp.where(gone, jnp.zeros((), BF16), kbuf[s])
         vbuf[s] = jnp.where(gone, jnp.zeros((), BF16), vbuf[s])
-        return 0
-
-    lax.fori_loop(0, cap, clear, 0)
-
-    pick = lax.broadcasted_iota(jnp.int32, (HEAD, 2 * HEAD), 0)
-    half = lax.broadcasted_iota(jnp.int32, (HEAD, 2 * HEAD), 1) >= HEAD
-    chooser = jnp.where(
-        half, jnp.where((pick == 3) | (pick == 4), 1.0, 0.0), jnp.where(pick < 3, 1.0, 0.0)
-    ).astype(BF16)
-    wait_bytes(recv_c.at[pl.ds(1, n - 1)], recv_sem.at[2])
-    spread = jnp.dot(
-        recv_c[:, 16:32].reshape(n * 16, HEAD), chooser, preferred_element_type=F32
-    )
-    for j in range(n):
-        asm[j * 32 : j * 32 + 16, :] = spread[j * 16 : j * 16 + 16, :HEAD]
-        asm[j * 32 + 16 : j * 32 + 32, :] = spread[j * 16 : j * 16 + 16, HEAD:]
+
+    out_k0 = pltpu.make_async_copy(kbuf.at[pl.ds(0, cap)], mk_hbm.at[pl.ds(0, cap)], out_sem.at[2])
+    out_v0 = pltpu.make_async_copy(vbuf.at[pl.ds(0, cap)], mv_hbm.at[pl.ds(0, cap)], out_sem.at[3])
+    out_k0.start()
+    out_v0.start()
+
+    wait_bytes(recv_m.at[pl.ds(1, n - 1)], recv_sem.at[10])
     peak = own_kv[0]
     for j in range(n):
+        row = jnp.broadcast_to(recv_m[j], (16, HEAD))
+        top = jnp.sum(jnp.where(lane16 == row16, row, 0.0), axis=1, keepdims=True)
+        amount = jnp.sum(jnp.where(lane16 == row16 + 16, row, 0.0), axis=1, keepdims=True)
+        asm[j * 32 : j * 32 + 16, :] = jnp.broadcast_to(top, (16, HEAD))
+        asm[j * 32 + 16 : j * 32 + 32, :] = jnp.broadcast_to(amount, (16, HEAD))
         peak = jnp.maximum(peak, asm[j * 32 : j * 32 + 16, :])
     own_scale = jnp.exp(own_kv[0] - peak)
     denominator = own_kv[1] * own_scale
@@ -388,33 +406,16 @@
     for j in range(n):
         scale = jnp.exp(asm[j * 32 : j * 32 + 16, :] - peak)
         denominator = denominator + asm[j * 32 + 16 : j * 32 + 32, :] * scale
-        numerator = numerator + recv_c[j, 0:16].astype(F32) * scale
+        asm[j * 32 : j * 32 + 16, :] = scale
+    wait_bytes(recv_c.at[pl.ds(1, n - 1)], recv_sem.at[2])
+    for j in range(n):
+        numerator = numerator + recv_c[j].astype(F32) * asm[j * 32 : j * 32 + 16, :]
     att_all[me] = (numerator / denominator).astype(BF16)
 
-    def send_attention(j, _):
-        peer = lax.rem(me + j, n)
+    for peer, _ in peers:
         remote(att_all.at[me], att_all.at[me], 3, "ctx", peer).start()
-        return 0
-
-    lax.fori_loop(1, n, send_attention, 0)
-
-    wait_bytes(kxy.at[pl.ds(0, ny - 1)], recv_sem.at[7])
-    wait_bytes(vxy.at[pl.ds(0, nx - 1)], recv_sem.at[8])
-
-    def source_of(mark):
-        index = jnp.maximum(mark - 1, 0)
-        device = jnp.right_shift(index, 1)
-        which = jnp.bitwise_and(index, 1)
-        src_core = lax.rem(device, nc)
-        src_y = lax.rem(device // nc, ny)
-        src_x = device // (nc * ny)
-        return src_x, src_y, src_core, which
-
-    for i in range(ARRIVALS):
-        src_x, src_y, _, which = source_of(tab_s[i, 4])
-        sib_send[0, i] = kxy[src_y, src_x, which]
-        sib_send[1, i] = vxy[src_x, src_y, which]
-    remote(sib_send, sib_recv, 9, "ctx", sibling).start()
+
+    second_hop(AFTER_QUERY + AFTER_BLOCKS, max(nx, ny))
 
     loads[4].wait()
     wait_bytes(att_all.at[pl.ds(0, n - 1)], recv_sem.at[3])
@@ -437,12 +438,27 @@
                 step * requests + t * rows_t : step * requests + (t + 1) * rows_t
             ]
 
-    def send_projected(j, _):
+    for j in far_first(tsize):
         peer = lax.rem(mt + j, tsize)
         remote(p_send.at[peer], p_recv.at[j], 4, "tp", peer).start()
-        return 0
-
-    lax.fori_loop(1, tsize, send_projected, 0)
+
+    wait_bytes(kxy.at[pl.ds(0, ny - 1)], recv_sem.at[7])
+    wait_bytes(vxy.at[pl.ds(0, nx - 1)], recv_sem.at[8])
+
+    def source_of(mark):
+        index = jnp.maximum(mark - 1, 0)
+        device = jnp.right_shift(index, 1)
+        which = jnp.bitwise_and(index, 1)
+        src_core = lax.rem(device, nc)
+        src_y = lax.rem(device // nc, ny)
+        src_x = device // (nc * ny)
+        return src_x, src_y, src_core, which
+
+    for i in range(ARRIVALS):
+        src_x, src_y, _, which = source_of(tab_s[i, 4])
+        sib_send[0, i] = kxy[src_y, src_x, which]
+        sib_send[1, i] = vxy[src_x, src_y, which]
+    remote(sib_send, sib_recv, 9, "ctx", sibling).start()
 
     wait_bytes(sib_recv, recv_sem.at[9])
     for i in range(ARRIVALS):
@@ -454,8 +470,9 @@
         kbuf[cap + i] = jnp.where(arrived, new_page, kbuf[cap + i])
         new_page = jnp.where(here, vxy[src_x, src_y, which], sib_recv[1, i])
         vbuf[cap + i] = jnp.where(arrived, new_page, vbuf[cap + i])
-    out_k = pltpu.make_async_copy(kbuf, mk_hbm, out_sem.at[0])
-    out_v = pltpu.make_async_copy(vbuf, mv_hbm, out_sem.at[1])
+    rest = pl.ds(cap, ARRIVALS)
+    out_k = pltpu.make_async_copy(kbuf.at[rest], mk_hbm.at[rest], out_sem.at[0])
+    out_v = pltpu.make_async_copy(vbuf.at[rest], mv_hbm.at[rest], out_sem.at[1])
     out_k.start()
     out_v.start()
 
@@ -484,8 +501,11 @@
     wait_bytes(kxy.at[pl.ds(0, ny - 1)], send_sem.at[7])
     wait_bytes(vxy.at[pl.ds(0, nx - 1)], send_sem.at[8])
     wait_bytes(sib_send, send_sem.at[9])
+    wait_bytes(recv_m.at[pl.ds(1, n - 1)], send_sem.at[10])
     out_k.wait()
     out_v.wait()
+    out_k0.wait()
+    out_v0.wait()
 
 
 def grid_of(n):
@@ -515,12 +535,8 @@
     cap = slots - ARRIVALS
     nx, ny, nc = grid_of(n)
     rows_t = requests // tsize
-    half = HEAD // 2
-    inverse = THETA ** (-(np.arange(half, dtype=np.float64) * 2.0 / HEAD))
-    inverse = np.concatenate([inverse, inverse])[None, :].astype(np.float32)
     rows_n = -(-max(cap, requests) // 8) * 8
     vmem = pl.BlockSpec(memory_space=pltpu.VMEM)
-    smem = pl.BlockSpec(memory_space=pltpu.SMEM)
     anywhere = pl.BlockSpec(memory_space=pl.ANY)
     out = pl.pallas_call(
         functools.partial(kernel, n, tsize, (nx, ny, nc), depth * n),
@@ -530,9 +546,16 @@
             jax.ShapeDtypeStruct(key_cache.shape, BF16),
             jax.ShapeDtypeStruct(value_cache.shape, BF16),
         ),
-        in_specs=[smem, smem] + [vmem] * 6 + [anywhere] * 5,
+        in_specs=[anywhere] * 12,
         out_specs=(vmem, vmem, anywhere, anywhere),
         scratch_shapes=[
+            pltpu.SMEM(lengths.shape, jnp.int32),
+            pltpu.SMEM(move_from.shape, jnp.int32),
+            pltpu.VMEM((1,) + move_to.shape, jnp.int32),
+            pltpu.VMEM(page_table.shape, jnp.int32),
+            pltpu.VMEM(x_first.shape, BF16),
+            pltpu.VMEM(x_second.shape, BF16),
+            pltpu.VMEM(norm_gain.shape, BF16),
             pltpu.VMEM(w_query.shape, BF16),
             pltpu.VMEM(key_value_weight.shape, BF16),
             pltpu.VMEM(w_out.shape, BF16),
@@ -546,10 +569,14 @@
             pltpu.VMEM((128, page_table.shape[1]), jnp.int32),
             pltpu.VMEM((rows_n, 128), jnp.int32),
             pltpu.SMEM((rows_n, 128), jnp.int32),
-            pltpu.VMEM((8, 48, HEAD), F32),
+            pltpu.VMEM((cap, 16, PAGE), F32),
+            pltpu.VMEM((cap, 16, PAGE), BF16),
+            pltpu.VMEM((cap, 48, HEAD), F32),
             pltpu.VMEM((cap + 1, 48, HEAD), F32),
-            pltpu.VMEM((n, 32, HEAD), BF16),
-            pltpu.VMEM((n, 32, HEAD), BF16),
+            pltpu.VMEM((n, 16, HEAD), BF16),
+            pltpu.VMEM((n, 16, HEAD), BF16),
+            pltpu.VMEM((n, 1, HEAD), F32),
+            pltpu.VMEM((n, 1, HEAD), F32),
             pltpu.VMEM((n, 16, HEAD), BF16),
             pltpu.VMEM((n * 16, HEAD), F32),
             pltpu.VMEM((tsize, 2 * rows_t, depth), F32),
@@ -558,32 +585,65 @@
             pltpu.VMEM((nx, ny, 2, PAGE, HEAD), BF16),
             pltpu.VMEM((2, ARRIVALS, PAGE, HEAD), BF16),
             pltpu.VMEM((2, ARRIVALS, PAGE, HEAD), BF16),
-            pltpu.SemaphoreType.DMA((5,)),
-            pltpu.SemaphoreType.DMA((2,)),
+            pltpu.SemaphoreType.DMA((12,)),
+            pltpu.SemaphoreType.DMA((4,)),
             pltpu.SemaphoreType.DMA,
-            pltpu.SemaphoreType.DMA((10,)),
-            pltpu.SemaphoreType.DMA((10,)),
+            pltpu.SemaphoreType.DMA((11,)),
+            pltpu.SemaphoreType.DMA((11,)),
         ],
         compiler_params=pltpu.CompilerParams(
-            collective_id=0, has_side_effects=True, vmem_limit_bytes=40 * 1024 * 1024
+            collective_id=0, has_side_effects=True, vmem_limit_bytes=VMEM_GRANT
         ),
         name="decode_two_steps",
     )(
         lengths,
         move_from,
-        move_to.reshape(1, -1),
+        move_to,
         page_table,
-        jnp.asarray(inverse),
         x_first,
         x_second,
-        norm_gain.reshape(1, -1),
+        norm_gain,
         w_query,
         key_value_weight,
         w_out,
         key_cache,
         value_cache,
     )
-    return out
+    def chunks(ref):
+        size = ref.shape[0]
+        step = -(-size // CHUNKS) if len(ref.shape) == 3 else size
+        return [(at, min(step, size - at)) for at in range(0, size, step)]
+
+    total = sum(len(chunks(o)) for o in out)
+
+    def store(*refs):
+        sources, targets, held = refs[:4], refs[4:8], refs[8:12]
+        in_sem, out_sem = refs[12], refs[13]
+        inward, outward = [], []
+        for a, b, c in zip(sources, targets, held):
+            for at, size in chunks(a):
+                k = len(inward)
+                cut = pl.ds(at, size)
+                inward.append(pltpu.make_async_copy(a.at[cut], c.at[cut], in_sem.at[k]))
+                outward.append(pltpu.make_async_copy(c.at[cut], b.at[cut], out_sem.at[k]))
+        for copy in inward:
+            copy.start()
+        for first, second in zip(inward, outward):
+            first.wait()
+            second.start()
+        for copy in outward:
+            copy.wait()
+
+    return pl.pallas_call(
+        store,
+        out_shape=tuple(jax.ShapeDtypeStruct(o.shape, o.dtype) for o in out),
+        in_specs=[anywhere] * 4,
+        out_specs=(anywhere,) * 4,
+        scratch_shapes=[pltpu.VMEM(o.shape, o.dtype) for o in out]
+        + [pltpu.SemaphoreType.DMA((total,))] * 2,
+        compiler_params=pltpu.CompilerParams(vmem_limit_bytes=VMEM_GRANT),
+        name="store_results",
+    )(*out)
 
 
 def solution(mesh):

time: 69.3 us -> 44.3 us (0.64)
  local copies, waits for them, and re-layouts: 14.4 us -> 0 us
  Pallas kernels: 53.7 us -> 43.5 us
    unnamed x28 -> x0, local copies, waits for them, and re-layouts: 13.8 us -> none
    pallas_call x1, Pallas kernels: 53.7 us -> 40.8 us  [per_device(): pl.pallas_call(functools.partial(kernel, n, tsize, (nx, ny, nc), depth *...]
    pallas_call x0 -> x1, Pallas kernels: none -> 2.71 us  [per_device(): pl.pallas_call(store, out_shape=tuple((jax.ShapeDtypeStruct(o.shape, o.dt...]
where the time goes in v2:
time: 44.3 us; the launch traced here: 44.1 us
  Pallas kernels  43.5 us (98%)
  between operations  0.64 us (1%)
    pallas_call x1, Pallas kernels, per_device(): pl.pallas_call(functools.partial(kernel, n, tsize, (nx, ny, nc), depth *...  40.8 us
    pallas_call x1, Pallas kernels, per_device(): pl.pallas_call(store, out_shape=tuple((jax.ShapeDtypeStruct(o.shape, o.dt...  2.71 us

profile of v2, /device:TPU:1, one launch (start us, length us, event | category | flops | bytes accessed | tf_op | source)
XLA Modules:
  0.0 44.1 jit_solution(2530124980861686385)
XLA Ops:
  0.6 40.8 %decode_two_steps.1 = (bf16[4,256]{1,0:T(4,128)(2,1)}, bf16[4,256]{1,0:T(4,128)(2,1)}, bf16[43,128,128]{2,1,0:T(8,128)(2,1)}, bf16[43,128,128]{2,1,0:T(8,128)(2,1)}) custom-call(s32[32]{0:T(128)} %lengths_hbm.1, s32[64]{0:T(128)} %from_hbm.1, s32[64]{0:T(128)} %to_hbm.1, s32[32,128]{1,0:T(8,128)} %table_hbm.1, bf16[32,256]{1,0:T(8,128)(2,1)} %x1_hbm.1, ...), custom_call_target="tpu_custom_call" | custom-call | tf_op jit(solution)/shard_map/decode_two_steps/pallas_call | solution.py:541
  41.4 2.7 %store_results.1 = (bf16[4,256]{1,0:T(4,128)(2,1)}, bf16[4,256]{1,0:T(4,128)(2,1)}, bf16[43,128,128]{2,1,0:T(8,128)(2,1)}, bf16[43,128,128]{2,1,0:T(8,128)(2,1)}) custom-call(bf16[4,256]{1,0:T(4,128)(2,1)} %get-tuple-element.8.refs_0_, bf16[4,256]{1,0:T(4,128)(2,1)} %get-tuple-element.9.refs_1_, bf16[43,128,128]{2,1,0:T(8,128)(2,1)} %get-tuple-element.10.refs_2_, ...), custom_call_target="tpu_custom_call" | custom-call | tf_op jit(solution)/shard_map/store_results/pallas_call | solution.py:637

commit v3 on v2

--- a/solution.py
+++ b/solution.py
@@ -19,9 +19,7 @@
 MESH = pl.DeviceIdType.MESH
 F32 = jnp.float32
 BF16 = jnp.bfloat16
-VMEM_GRANT = 58 * 1024 * 1024
-AFTER_QUERY, AFTER_BLOCKS = 2, 1
-CHUNKS = 4
+VMEM_GRANT = 24 * 1024 * 1024
 
 TURN_HIGH = 6.28125
 TURN_MID = float(np.float32(np.round((2 * np.pi - TURN_HIGH) * 2.0**20) / 2.0**20))
@@ -36,6 +34,82 @@
 def split2(v):
     high = v.astype(BF16).astype(F32)
     return high, v - high
+
+
+class PageRing:
+    def __init__(self, held, r, c, peer_r, peer_c, send_sem, recv_sem):
+        self.held, self.r, self.c = held, r, c
+        self.peer_r, self.peer_c = peer_r, peer_c
+        self.send_sem, self.recv_sem = send_sem, recv_sem
+        self.rows, self.columns = held.shape[0], held.shape[1]
+        self.sides_r = [1, -1] if self.rows == 4 else [1]
+        self.sides_c = [1, -1] if self.columns == 4 else [1]
+        self.near = [0] + self.sides_c
+        self.far = [2] if self.columns == 4 else []
+        count_r = len(self.sides_r)
+        relayed = self.rows == 4
+        self.blocks = [
+            len(self.sides_c),
+            len(self.far),
+            len(self.near) * count_r,
+            len(self.far) * count_r,
+            len(self.near) * relayed,
+            len(self.far) * relayed,
+        ]
+
+    def row(self, d):
+        return lax.rem(self.r + d + self.rows, self.rows)
+
+    def column(self, d):
+        return lax.rem(self.c + d + self.columns, self.columns)
+
+    def send(self, stage, ref, peer):
+        pltpu.make_async_remote_copy(
+            src_ref=ref,
+            dst_ref=ref,
+            send_sem=self.send_sem.at[stage],
+            recv_sem=self.recv_sem.at[stage],
+            device_id={"ctx": peer},
+            device_id_type=MESH,
+        ).start()
+
+    def wait(self, sem, stage):
+        count = self.blocks[stage]
+        if not count:
+            return
+        wide = max(w for w in range(1, self.columns + 1) if count % w == 0)
+        ref = self.held.at[pl.ds(0, count // wide), pl.ds(0, wide)]
+        pltpu.make_async_copy(ref, ref, sem.at[stage]).wait()
+
+    def arrived(self, stage):
+        self.wait(self.recv_sem, stage)
+
+    def left(self):
+        for stage in range(6):
+            self.wait(self.send_sem, stage)
+
+    def first_near(self):
+        for d in self.sides_c:
+            self.send(0, self.held.at[self.r, self.c], self.peer_c(d))
+
+    def first_far(self):
+        self.arrived(0)
+        for _ in self.far:
+            for page, d in enumerate(self.sides_c):
+                self.send(1, self.held.at[self.r, self.column(-d), page], self.peer_c(d))
+
+    def second_near(self, stage, columns):
+        for e in columns:
+            for d in self.sides_r:
+                self.send(stage, self.held.at[self.r, self.column(e)], self.peer_r(d))
+
+    def second_far(self, stage, columns):
+        if self.rows == 4:
+            for e in columns:
+                for page, d in enumerate(self.sides_r):
+                    self.send(
+                        stage, self.held.at[self.row(-d), self.column(e), page], self.peer_r(d)
+                    )
 
 
 def kernel(
@@ -57,8 +131,8 @@
     vc_hbm,
     o1_v,
     o2_v,
-    mk_hbm,
-    mv_hbm,
+    kbuf,
+    vbuf,
     lengths_s,
     from_s,
     to_v,
@@ -69,13 +143,15 @@
     wq,
     wkv,
     wo,
-    kbuf,
-    vbuf,
     asm,
+    asm_kv,
+    send_s,
+    recv_s,
+    send_kv,
+    recv_kv,
     send_a,
     recv_a,
     q_all,
-    own_kv,
     slots_t,
     tab_v,
     tab_s,
@@ -89,6 +165,7 @@
     recv_m,
     att_all,
     att_f,
+    p_part,
     p_send,
     p_recv,
     kxy,
@@ -96,10 +173,11 @@
     sib_send,
     sib_recv,
     load_sem,
-    out_sem,
     tab_sem,
     send_sem,
     recv_sem,
+    page_send,
+    page_recv,
 ):
     nx, ny, nc = grid_xyc
     me = lax.axis_index("ctx")
@@ -112,6 +190,7 @@
     slots = kbuf.shape[0]
     cap = slots - ARRIVALS
     rows_t = requests // tsize
+    depth = x1_v.shape[1]
 
     loads = [
         pltpu.make_async_copy(src, dst, load_sem.at[i])
@@ -132,9 +211,6 @@
             ]
         )
     ]
-    for at in (5, 6, 7, 1, 0, 2, 3, 8, 9, 10, 11, 4):
-        loads[at].start()
-
     def hops(d, size):
         return min(d, size - d)
 
@@ -155,6 +231,8 @@
 
     for peer, _ in peers:
         pl.semaphore_signal(barrier, inc=1, device_id={"ctx": peer}, device_id_type=MESH)
+    for at in (5, 6, 7, 1, 0, 2, 3, 8, 9, 10, 11, 4):
+        loads[at].start()
     for j in far_first(tsize):
         pl.semaphore_signal(
             barrier, inc=1, device_id={"tp": lax.rem(mt + j, tsize)}, device_id_type=MESH
@@ -178,30 +256,32 @@
     x_both = jnp.concatenate([x1_v[...], x2_v[...]], axis=0).astype(F32)
     squares = jnp.sum(x_both * x_both, axis=1, keepdims=True)
     scaled = (x_both * gain_v[...].astype(F32)[None, :]).astype(BF16)
-    sq_high, sq_low = split2(jnp.broadcast_to(squares, (2 * requests, HEAD)))
-    loads[0].wait()
+    lane_r = lax.broadcasted_iota(jnp.int32, (requests, HEAD), 1)
+    both = jnp.where(lane_r < HEAD // 2, squares[:requests], squares[requests:])
+    for r in range(requests):
+        send_s[r] = both[r : r + 1]
     loads[1].wait()
-    for step in range(2):
-        rows = slice(step * requests, (step + 1) * requests)
-        asm[pl.ds(20 + step, requests, stride=32), :] = sq_high[rows]
-        asm[pl.ds(22 + step, requests, stride=32), :] = sq_low[rows]
     kv_part = jnp.dot(scaled, wkv[...], preferred_element_type=F32)
     for step in range(2):
         rows = slice(step * requests, (step + 1) * requests)
-        asm[pl.ds(16 + step, requests, stride=32), :] = kv_part[rows, :HEAD]
-        asm[pl.ds(18 + step, requests, stride=32), :] = kv_part[rows, HEAD:]
+        asm_kv[pl.ds(step, requests, stride=8), :] = kv_part[rows, :HEAD]
+        asm_kv[pl.ds(2 + step, requests, stride=8), :] = kv_part[rows, HEAD:]
+    loads[0].wait()
     for h in range(GROUP):
         part = jnp.dot(scaled, wq[:, h * HEAD : (h + 1) * HEAD], preferred_element_type=F32)
         for step in range(2):
             rows = slice(step * requests, (step + 1) * requests)
-            asm[pl.ds(step * GROUP + h, requests, stride=32), :] = part[rows]
+            asm[pl.ds(step * GROUP + h, requests, stride=16), :] = part[rows]
 
     for r in range(requests):
-        send_a[r] = asm[r * 32 : r * 32 + 32, :].astype(BF16)
+        send_a[r] = asm[r * 16 : r * 16 + 16, :].astype(BF16)
     pl.semaphore_wait(barrier, n - 1 + tsize - 1)
 
     for peer, at in peers:
+        remote(send_s.at[peer], recv_s.at[at], 11, "ctx", peer).start()
         remote(send_a.at[peer], recv_a.at[at], 0, "ctx", peer).start()
+    for r in range(requests):
+        send_kv[r] = asm_kv[r * 8 : r * 8 + 4, :]
 
     for at in (2, 3, 8, 9, 10, 11):
         loads[at].wait()
@@ -209,12 +289,18 @@
         leaving = jnp.clip(from_s[2 * me + i] - me * slots, 0, slots - 1)
         kxy[yi, xi, i] = kbuf[leaving]
         vxy[xi, yi, i] = vbuf[leaving]
-    for d in far_first(nx):
-        peer = (lax.rem(xi + d, nx) * ny + yi) * nc + core
-        remote(kxy.at[yi, xi], kxy.at[yi, xi], 5, "ctx", peer).start()
-    for d in far_first(ny):
-        peer = (xi * ny + lax.rem(yi + d, ny)) * nc + core
-        remote(vxy.at[xi, yi], vxy.at[xi, yi], 6, "ctx", peer).start()
+    def peer_x(d):
+        return (lax.rem(xi + d + nx, nx) * ny + yi) * nc + core
+
+    def peer_y(d):
+        return (xi * ny + lax.rem(yi + d + ny, ny)) * nc + core
+
+    rings = [
+        PageRing(kxy, yi, xi, peer_y, peer_x, page_send.at[0], page_recv.at[0]),
+        PageRing(vxy, xi, yi, peer_x, peer_y, page_send.at[1], page_recv.at[1]),
+    ]
+    for ring in rings:
+        ring.first_near()
 
     local_table = table_v[...] - me * slots
     code = (
@@ -276,53 +362,33 @@
         )
 
     tab_copy.wait()
-    total = asm[pl.ds(pl.multiple_of(me * 32, 32), 32), :]
+    square = send_s[me]
+    wait_bytes(recv_s.at[pl.ds(1, n - 1)], recv_sem.at[11])
+    for j in range(1, n):
+        square = square + recv_s[j]
+    rms = lax.rsqrt(square / width + EPSILON)
+    turned = pltpu.roll(rms, HEAD // 2, 1)
+    rms = jnp.concatenate(
+        [jnp.where(lane < HEAD // 2, rms, turned), jnp.where(lane < HEAD // 2, turned, rms)], axis=0
+    )
+    cosine_16, sine_16 = by_step(cosine * rms, GROUP), by_step(sine * rms, GROUP)
+    total = asm[pl.ds(pl.multiple_of(me * 16, 16), 16), :]
     wait_bytes(recv_a.at[pl.ds(1, n - 1)], recv_sem.at[0])
     for j in range(1, n):
         total = total + recv_a[j].astype(F32)
-    square = total[20:22] + total[22:24]
-    rms = lax.rsqrt(square / width + EPSILON)
-
-    def rotated(v, count):
-        return v * by_step(cosine, count) + pltpu.roll(v, HEAD // 2, 1) * by_step(sine, count)
-
-    q_own = rotated(total[:16] * by_step(rms, GROUP), GROUP).astype(BF16)
+    q_own = (total * cosine_16 + pltpu.roll(total, HEAD // 2, 1) * sine_16).astype(BF16)
     q_all[me] = q_own
 
     for peer, _ in peers:
         remote(q_all.at[me], q_all.at[me], 1, "ctx", peer).start()
 
-    wait_bytes(kxy.at[0, pl.ds(0, nx - 1)], recv_sem.at[5])
-    wait_bytes(vxy.at[0, pl.ds(0, ny - 1)], recv_sem.at[6])
-
-    def second_hop(first, last):
-        for part in range(first, min(last, nx)):
-            for d in far_first(ny):
-                peer = (xi * ny + lax.rem(yi + d, ny)) * nc + core
-                remote(kxy.at[yi, part], kxy.at[yi, part], 7, "ctx", peer).start()
-        for part in range(first, min(last, ny)):
-            for d in far_first(nx):
-                peer = (lax.rem(xi + d, nx) * ny + yi) * nc + core
-                remote(vxy.at[xi, part], vxy.at[xi, part], 8, "ctx", peer).start()
-
-    second_hop(0, AFTER_QUERY)
-
-    new_k = rotated(total[16:18] * rms, 1).astype(BF16).astype(F32)
-    new_v = (total[18:20] * rms).astype(BF16).astype(F32)
-    qf = q_own.astype(F32)
-    second = lax.broadcasted_iota(jnp.int32, (16, HEAD), 0) >= GROUP
-    own_1 = jnp.sum(qf * new_k[0:1], axis=1, keepdims=True) * SCALE
-    own_2 = jnp.sum(qf * new_k[1:2], axis=1, keepdims=True) * SCALE
-    own_1 = jnp.broadcast_to(own_1, (16, HEAD))
-    own_2 = jnp.where(second, jnp.broadcast_to(own_2, (16, HEAD)), NEGATIVE)
-    own_max = jnp.maximum(own_1, own_2)
-    own_w1 = jnp.exp(own_1 - own_max).astype(BF16).astype(F32)
-    own_w2 = jnp.exp(own_2 - own_max).astype(BF16).astype(F32)
-    own_total = own_w1 + own_w2
-    own_out = own_w1 * new_v[0:1] + own_w2 * new_v[1:2]
-    own_kv[0] = own_max
-    own_kv[1] = own_total
-    own_kv[2] = own_out
+    for peer, at in peers:
+        remote(send_kv.at[peer], recv_kv.at[at], 12, "ctx", peer).start()
+
+    for ring in rings:
+        ring.first_far()
+    for ring in rings:
+        ring.second_near(2, ring.near)
 
     scan[0, 0:16] = jnp.full((16, HEAD), NEGATIVE, F32)
     scan[0, 16:48] = jnp.zeros((32, HEAD), F32)
@@ -365,18 +431,47 @@
 
     lane16 = lax.broadcasted_iota(jnp.int32, (16, HEAD), 1)
     row16 = lax.broadcasted_iota(jnp.int32, (16, HEAD), 0)
-    for r in range(requests):
-        at = tab_s[r, 2]
-        send_c[r] = scan[at, 32:48].astype(BF16)
-        both = jnp.where(lane16 == row16 + 16, scan[at, 16:32], 0.0)
-        both = jnp.where(lane16 == row16, scan[at, 0:16], both)
-        send_m[r] = jnp.sum(both, axis=0, keepdims=True)
+
+    def as_row(v, chosen):
+        return jnp.sum(jnp.where(chosen, v, 0.0), axis=0, keepdims=True)
+
+    for peer, at in peers + [(me, 0)]:
+        source = tab_s[peer, 2]
+        chosen = lane16 == row16 + at % 8 * 16
+        out_c = send_c if at else recv_c
+        out_m = send_m if at else recv_m
+        out_c[at] = scan[source, 32:48].astype(BF16)
+        out_m[at, 0:1] = as_row(scan[source, 0:16], chosen)
+        out_m[at, 1:2] = as_row(scan[source, 16:32], chosen)
     for peer, at in peers:
-        remote(send_m.at[peer], recv_m.at[at], 10, "ctx", peer).start()
-        remote(send_c.at[peer], recv_c.at[at], 2, "ctx", peer).start()
-    recv_c[0] = send_c[me]
-    recv_m[0] = send_m[me]
-    second_hop(AFTER_QUERY, AFTER_QUERY + AFTER_BLOCKS)
+        remote(send_m.at[at], recv_m.at[at], 10, "ctx", peer).start()
+        remote(send_c.at[at], recv_c.at[at], 2, "ctx", peer).start()
+    for ring in rings:
+        ring.arrived(1)
+        ring.second_near(3, ring.far)
+    for ring in rings:
+        ring.arrived(2)
+        ring.second_far(4, ring.near)
+
+    new = asm_kv[pl.ds(pl.multiple_of(me * 8, 8), 4), :]
+    wait_bytes(recv_kv.at[pl.ds(1, n - 1)], recv_sem.at[12])
+    for j in range(1, n):
+        new = new + recv_kv[j]
+    new_k = new[0:2] * rms
+    new_k = (new_k * cosine + pltpu.roll(new_k, HEAD // 2, 1) * sine).astype(BF16).astype(F32)
+    new_v = (new[2:4] * rms).astype(BF16).astype(F32)
+    qf = q_own.astype(F32)
+    own_1 = jnp.sum(qf * new_k[0:1], axis=1, keepdims=True) * SCALE
+    own_2 = jnp.sum(qf * new_k[1:2], axis=1, keepdims=True) * SCALE
+    own_1 = jnp.broadcast_to(own_1, (16, HEAD))
+    own_2 = jnp.where(row16 >= GROUP, jnp.broadcast_to(own_2, (16, HEAD)), NEGATIVE)
+    own_max = jnp.maximum(own_1, own_2)
+    own_w1 = jnp.exp(own_1 - own_max).astype(BF16).astype(F32)
+    own_w2 = jnp.exp(own_2 - own_max).astype(BF16).astype(F32)
+    own_out = own_w1 * new_v[0:1] + own_w2 * new_v[1:2]
+    repeated = lane16 % 16 == row16
+    own_max_row = as_row(own_max, repeated)
+    own_total_row = as_row(own_w1 + own_w2, repeated)
 
     leave_0 = from_s[2 * me] - me * slots
     leave_1 = from_s[2 * me + 1] - me * slots
@@ -386,36 +481,49 @@
         kbuf[s] = jnp.where(gone, jnp.zeros((), BF16), kbuf[s])
         vbuf[s] = jnp.where(gone, jnp.zeros((), BF16), vbuf[s])
 
-    out_k0 = pltpu.make_async_copy(kbuf.at[pl.ds(0, cap)], mk_hbm.at[pl.ds(0, cap)], out_sem.at[2])
-    out_v0 = pltpu.make_async_copy(vbuf.at[pl.ds(0, cap)], mv_hbm.at[pl.ds(0, cap)], out_sem.at[3])
-    out_k0.start()
-    out_v0.start()
+    def over_groups(v, combine):
+        for shift in (16, 32, 64):
+            v = combine(v, pltpu.roll(v, shift, 1))
+        return v
 
     wait_bytes(recv_m.at[pl.ds(1, n - 1)], recv_sem.at[10])
-    peak = own_kv[0]
-    for j in range(n):
-        row = jnp.broadcast_to(recv_m[j], (16, HEAD))
-        top = jnp.sum(jnp.where(lane16 == row16, row, 0.0), axis=1, keepdims=True)
-        amount = jnp.sum(jnp.where(lane16 == row16 + 16, row, 0.0), axis=1, keepdims=True)
-        asm[j * 32 : j * 32 + 16, :] = jnp.broadcast_to(top, (16, HEAD))
-        asm[j * 32 + 16 : j * 32 + 32, :] = jnp.broadcast_to(amount, (16, HEAD))
-        peak = jnp.maximum(peak, asm[j * 32 : j * 32 + 16, :])
-    own_scale = jnp.exp(own_kv[0] - peak)
-    denominator = own_kv[1] * own_scale
-    numerator = own_kv[2] * own_scale
-    for j in range(n):
-        scale = jnp.exp(asm[j * 32 : j * 32 + 16, :] - peak)
-        denominator = denominator + asm[j * 32 + 16 : j * 32 + 32, :] * scale
-        asm[j * 32 : j * 32 + 16, :] = scale
+    tops, amounts = [], []
+    for k in range(n // 8):
+        rows = recv_m[8 * k]
+        for j in range(8 * k + 1, 8 * k + 8):
+            rows = rows + recv_m[j]
+        tops.append(rows[0:1])
+        amounts.append(rows[1:2])
+    peak = over_groups(functools.reduce(jnp.maximum, tops), jnp.maximum)
+    peak = jnp.maximum(peak, own_max_row)
+    scales = [jnp.exp(top - peak) for top in tops]
+    own_scale = jnp.exp(own_max_row - peak)
+    denominator = sum(a * b for a, b in zip(amounts, scales))
+    denominator = over_groups(denominator, jnp.add) + own_total_row * own_scale
+    inverse_total = 1.0 / denominator
+    shares = jnp.concatenate(
+        [
+            jnp.where(repeated, jnp.broadcast_to(scale * inverse_total, (16, HEAD)), 0.0)
+            for scale in scales
+        ],
+        axis=1,
+    )
+    share_high, share_low = split2(shares)
+    share_both = jnp.concatenate([share_high, share_low], axis=0).astype(BF16)
+    own_share = jnp.broadcast_to(own_scale * inverse_total, (16, HEAD))
+    own_share = jnp.sum(jnp.where(lane16 == row16, own_share, 0.0), axis=1, keepdims=True)
     wait_bytes(recv_c.at[pl.ds(1, n - 1)], recv_sem.at[2])
-    for j in range(n):
-        numerator = numerator + recv_c[j].astype(F32) * asm[j * 32 : j * 32 + 16, :]
-    att_all[me] = (numerator / denominator).astype(BF16)
+    mixed = jnp.dot(
+        share_both, recv_c[...].reshape(n * 16, HEAD), preferred_element_type=F32
+    )
+    att_all[me] = (mixed[:16] + mixed[16:] + own_out * own_share).astype(BF16)
 
     for peer, _ in peers:
         remote(att_all.at[me], att_all.at[me], 3, "ctx", peer).start()
 
-    second_hop(AFTER_QUERY + AFTER_BLOCKS, max(nx, ny))
+    for ring in rings:
+        ring.arrived(3)
+        ring.second_far(5, ring.far)
 
     loads[4].wait()
     wait_bytes(att_all.at[pl.ds(0, n - 1)], recv_sem.at[3])
@@ -432,18 +540,24 @@
         axis=0,
     ).astype(BF16)
     projected = jnp.dot(attention, wo[...], preferred_element_type=F32)
+    wide = depth // 2
     for t in range(tsize):
         for step in range(2):
-            p_send[t, step * rows_t : (step + 1) * rows_t] = projected[
-                step * requests + t * rows_t : step * requests + (t + 1) * rows_t
-            ]
-
+            first = step * requests + t * rows_t
+            for side in range(2):
+                at = side * 2 * rows_t + step * rows_t
+                p_part[t, at : at + rows_t] = projected[
+                    first : first + rows_t, side * wide : (side + 1) * wide
+                ]
+    for t in range(tsize):
+        p_send[t] = p_part[t].astype(BF16)
     for j in far_first(tsize):
         peer = lax.rem(mt + j, tsize)
         remote(p_send.at[peer], p_recv.at[j], 4, "tp", peer).start()
 
-    wait_bytes(kxy.at[pl.ds(0, ny - 1)], recv_sem.at[7])
-    wait_bytes(vxy.at[pl.ds(0, nx - 1)], recv_sem.at[8])
+    for ring in rings:
+        ring.arrived(4)
+        ring.arrived(5)
 
     def source_of(mark):
         index = jnp.maximum(mark - 1, 0)
@@ -470,12 +584,6 @@
         kbuf[cap + i] = jnp.where(arrived, new_page, kbuf[cap + i])
         new_page = jnp.where(here, vxy[src_x, src_y, which], sib_recv[1, i])
         vbuf[cap + i] = jnp.where(arrived, new_page, vbuf[cap + i])
-    rest = pl.ds(cap, ARRIVALS)
-    out_k = pltpu.make_async_copy(kbuf.at[rest], mk_hbm.at[rest], out_sem.at[0])
-    out_v = pltpu.make_async_copy(vbuf.at[rest], mv_hbm.at[rest], out_sem.at[1])
-    out_k.start()
-    out_v.start()
-
     residual_1 = jnp.zeros((rows_t, x1_v.shape[1]), F32)
     residual_2 = residual_1
     x1_f, x2_f = x1_v[...].astype(F32), x2_v[...].astype(F32)
@@ -485,9 +593,10 @@
         residual_2 = jnp.where(mt == t, x2_f[rows], residual_2)
 
     wait_bytes(p_recv.at[pl.ds(1, tsize - 1)], recv_sem.at[4])
-    summed = p_send[mt]
+    summed = p_part[mt]
     for j in range(1, tsize):
-        summed = summed + p_recv[j]
+        summed = summed + p_recv[j].astype(F32)
+    summed = jnp.concatenate([summed[: 2 * rows_t], summed[2 * rows_t :]], axis=1)
     o1_v[...] = (residual_1 + summed[:rows_t]).astype(BF16)
     o2_v[...] = (residual_2 + summed[rows_t:]).astype(BF16)
 
@@ -496,16 +605,12 @@
     wait_bytes(recv_c.at[pl.ds(1, n - 1)], send_sem.at[2])
     wait_bytes(att_all.at[pl.ds(0, n - 1)], send_sem.at[3])
     wait_bytes(p_recv.at[pl.ds(1, tsize - 1)], send_sem.at[4])
-    wait_bytes(kxy.at[0, pl.ds(0, nx - 1)], send_sem.at[5])
-    wait_bytes(vxy.at[0, pl.ds(0, ny - 1)], send_sem.at[6])
-    wait_bytes(kxy.at[pl.ds(0, ny - 1)], send_sem.at[7])
-    wait_bytes(vxy.at[pl.ds(0, nx - 1)], send_sem.at[8])
+    for ring in rings:
+        ring.left()
     wait_bytes(sib_send, send_sem.at[9])
     wait_bytes(recv_m.at[pl.ds(1, n - 1)], send_sem.at[10])
-    out_k.wait()
-    out_v.wait()
-    out_k0.wait()
-    out_v0.wait()
+    wait_bytes(recv_s.at[pl.ds(1, n - 1)], send_sem.at[11])
+    wait_bytes(recv_kv.at[pl.ds(1, n - 1)], send_sem.at[12])
 
 
 def grid_of(n):
@@ -541,13 +646,13 @@
     out = pl.pallas_call(
         functools.partial(kernel, n, tsize, (nx, ny, nc), depth * n),
         out_shape=(
-            jax.ShapeDtypeStruct((rows_t, depth), BF16),
-            jax.ShapeDtypeStruct((rows_t, depth), BF16),
-            jax.ShapeDtypeStruct(key_cache.shape, BF16),
-            jax.ShapeDtypeStruct(value_cache.shape, BF16),
+            pltpu.VMEM((rows_t, depth), BF16),
+            pltpu.VMEM((rows_t, depth), BF16),
+            pltpu.VMEM(key_cache.shape, BF16),
+            pltpu.VMEM(value_cache.shape, BF16),
         ),
         in_specs=[anywhere] * 12,
-        out_specs=(vmem, vmem, anywhere, anywhere),
+        out_specs=(vmem,) * 4,
         scratch_shapes=[
             pltpu.SMEM(lengths.shape, jnp.int32),
             pltpu.SMEM(move_from.shape, jnp.int32),
@@ -559,13 +664,15 @@
             pltpu.VMEM(w_query.shape, BF16),
             pltpu.VMEM(key_value_weight.shape, BF16),
             pltpu.VMEM(w_out.shape, BF16),
-            pltpu.VMEM(key_cache.shape, BF16),
-            pltpu.VMEM(value_cache.shape, BF16),
-            pltpu.VMEM((n * 32, HEAD), F32),
-            pltpu.VMEM((n, 32, HEAD), BF16),
-            pltpu.VMEM((n, 32, HEAD), BF16),
+            pltpu.VMEM((n * 16, HEAD), F32),
+            pltpu.VMEM((n * 8, HEAD), F32),
+            pltpu.VMEM((n, 1, HEAD), F32),
+            pltpu.VMEM((n, 1, HEAD), F32),
+            pltpu.VMEM((n, 4, HEAD), F32),
+            pltpu.VMEM((n, 4, HEAD), F32),
             pltpu.VMEM((n, 16, HEAD), BF16),
-            pltpu.VMEM((3, 16, HEAD), F32),
+            pltpu.VMEM((n, 16, HEAD), BF16),
+            pltpu.VMEM((n, 16, HEAD), BF16),
             pltpu.VMEM((128, page_table.shape[1]), jnp.int32),
             pltpu.VMEM((rows_n, 128), jnp.int32),
             pltpu.SMEM((rows_n, 128), jnp.int32),
@@ -575,63 +682,54 @@
             pltpu.VMEM((cap + 1, 48, HEAD), F32),
             pltpu.VMEM((n, 16, HEAD), BF16),
             pltpu.VMEM((n, 16, HEAD), BF16),
-            pltpu.VMEM((n, 1, HEAD), F32),
-            pltpu.VMEM((n, 1, HEAD), F32),
+            pltpu.VMEM((n, 2, HEAD), F32),
+            pltpu.VMEM((n, 2, HEAD), F32),
             pltpu.VMEM((n, 16, HEAD), BF16),
             pltpu.VMEM((n * 16, HEAD), F32),
-            pltpu.VMEM((tsize, 2 * rows_t, depth), F32),
-            pltpu.VMEM((tsize, 2 * rows_t, depth), F32),
+            pltpu.VMEM((tsize, 4 * rows_t, depth // 2), F32),
+            pltpu.VMEM((tsize, 4 * rows_t, depth // 2), BF16),
+            pltpu.VMEM((tsize, 4 * rows_t, depth // 2), BF16),
             pltpu.VMEM((ny, nx, 2, PAGE, HEAD), BF16),
             pltpu.VMEM((nx, ny, 2, PAGE, HEAD), BF16),
             pltpu.VMEM((2, ARRIVALS, PAGE, HEAD), BF16),
             pltpu.VMEM((2, ARRIVALS, PAGE, HEAD), BF16),
             pltpu.SemaphoreType.DMA((12,)),
-            pltpu.SemaphoreType.DMA((4,)),
             pltpu.SemaphoreType.DMA,
-            pltpu.SemaphoreType.DMA((11,)),
-            pltpu.SemaphoreType.DMA((11,)),
+            pltpu.SemaphoreType.DMA((13,)),
+            pltpu.SemaphoreType.DMA((13,)),
+            pltpu.SemaphoreType.DMA((2, 6)),
+            pltpu.SemaphoreType.DMA((2, 6)),
         ],
         compiler_params=pltpu.CompilerParams(
             collective_id=0, has_side_effects=True, vmem_limit_bytes=VMEM_GRANT
         ),
         name="decode_two_steps",
     )(
-        lengths,
-        move_from,
-        move_to,
-        page_table,
-        x_first,
-        x_second,
-        norm_gain,
-        w_query,
-        key_value_weight,
-        w_out,
-        key_cache,
-        value_cache,
-    )
-    def chunks(ref):
-        size = ref.shape[0]
-        step = -(-size // CHUNKS) if len(ref.shape) == 3 else size
-        return [(at, min(step, size - at)) for at in range(0, size, step)]
-
-    total = sum(len(chunks(o)) for o in out)
+        *(
+            pltpu.with_memory_space_constraint(x, pltpu.HBM)
+            for x in (
+                lengths,
+                move_from,
+                move_to,
+                page_table,
+                x_first,
+                x_second,
+                norm_gain,
+                w_query,
+                key_value_weight,
+                w_out,
+                key_cache,
+                value_cache,
+            )
+        )
+    )
 
     def store(*refs):
-        sources, targets, held = refs[:4], refs[4:8], refs[8:12]
-        in_sem, out_sem = refs[12], refs[13]
-        inward, outward = [], []
-        for a, b, c in zip(sources, targets, held):
-            for at, size in chunks(a):
-                k = len(inward)
-                cut = pl.ds(at, size)
-                inward.append(pltpu.make_async_copy(a.at[cut], c.at[cut], in_sem.at[k]))
-                outward.append(pltpu.make_async_copy(c.at[cut], b.at[cut], out_sem.at[k]))
-        for copy in inward:
+        sem = refs[8]
+        copies = [pltpu.make_async_copy(refs[i], refs[4 + i], sem.at[i]) for i in range(4)]
+        for copy in copies:
             copy.start()
-        for first, second in zip(inward, outward):
-            first.wait()
-            second.start()
-        for copy in outward:
+        for copy in copies:
             copy.wait()
 
     return pl.pallas_call(
@@ -639,8 +737,7 @@
         out_shape=tuple(jax.ShapeDtypeStruct(o.shape, o.dtype) for o in out),
         in_specs=[anywhere] * 4,
         out_specs=(anywhere,) * 4,
-        scratch_shapes=[pltpu.VMEM(o.shape, o.dtype) for o in out]
-        + [pltpu.SemaphoreType.DMA((total,))] * 2,
+        scratch_shapes=[pltpu.SemaphoreType.DMA((4,))],
         compiler_params=pltpu.CompilerParams(vmem_limit_bytes=VMEM_GRANT),
         name="store_results",
     )(*out)

time: 44.3 us -> 40.5 us (0.914)
  Pallas kernels: 43.5 us -> 39.7 us
    pallas_call x1, Pallas kernels: 40.8 us -> 38.1 us  [per_device(): pl.pallas_call(functools.partial(kernel, n, tsize, (nx, ny, nc), depth *...]
    pallas_call x1, Pallas kernels: 2.71 us -> 1.6 us  [per_device(): pl.pallas_call(store, out_shape=tuple((jax.ShapeDtypeStruct(o.shape, o.dt...]
where the time goes in v3:
time: 40.5 us; the launch traced here: 40.3 us
  Pallas kernels  39.7 us (98%)
  between operations  0.64 us (2%)
    pallas_call x1, Pallas kernels, per_device(): pl.pallas_call(functools.partial(kernel, n, tsize, (nx, ny, nc), depth *...  38.1 us
    pallas_call x1, Pallas kernels, per_device(): pl.pallas_call(store, out_shape=tuple((jax.ShapeDtypeStruct(o.shape, o.dt...  1.6 us

profile of v3, /device:TPU:1, one launch (start us, length us, event | category | flops | bytes accessed | tf_op | source)
XLA Modules:
  0.0 40.3 jit_solution(10242648211851244457)
XLA Ops:
  0.6 38.1 %decode_two_steps.1 = (bf16[4,256]{1,0:T(4,128)(2,1)S(1)}, bf16[4,256]{1,0:T(4,128)(2,1)S(1)}, bf16[43,128,128]{2,1,0:T(8,128)(2,1)S(1)}, bf16[43,128,128]{2,1,0:T(8,128)(2,1)S(1)}) custom-call(s32[32]{0:T(128)} %lengths_hbm.1, s32[64]{0:T(128)} %from_hbm.1, s32[64]{0:T(128)} %to_hbm.1, s32[32,128]{1,0:T(8,128)} %table_hbm.1, bf16[32,256]{1,0:T(8,128)(2,1)} %x1_hbm.1, ...), custom_call_target="tpu_custom_call" | custom-call | tf_op jit(solution)/shard_map/decode_two_steps/pallas_call | solution.py:646
  38.7 1.6 %store_results.1 = (bf16[4,256]{1,0:T(4,128)(2,1)}, bf16[4,256]{1,0:T(4,128)(2,1)}, bf16[43,128,128]{2,1,0:T(8,128)(2,1)}, bf16[43,128,128]{2,1,0:T(8,128)(2,1)}) custom-call(bf16[4,256]{1,0:T(4,128)(2,1)S(1)} %get-tuple-element.8.refs_0_, bf16[4,256]{1,0:T(4,128)(2,1)S(1)} %get-tuple-element.9.refs_1_, bf16[43,128,128]{2,1,0:T(8,128)(2,1)S(1)} %get-tuple-element.10.refs_2_, ...), custom_call_target="tpu_custom_call" | custom-call | tf_op jit(solution)/shard_map/store_results/pallas_call | solution.py:735

commit v4 on v3

--- a/solution.py
+++ b/solution.py
@@ -155,6 +155,8 @@
     slots_t,
     tab_v,
     tab_s,
+    kt,
+    valid,
     scores,
     weights,
     blocks,
@@ -301,6 +303,8 @@
     ]
     for ring in rings:
         ring.first_near()
+    for ring in rings:
+        ring.second_near(2, [0])
 
     local_table = table_v[...] - me * slots
     code = (
@@ -337,7 +341,10 @@
         jnp.where(targets - sibling * slots == move_row, move_lane + 1, 0), axis=1, keepdims=True
     )
     packed = jnp.zeros(wide, jnp.int32)
-    for i, column in enumerate([code_col, prev_col, last_col, arrive_col, arrive_sib]):
+    owner_safe = jnp.maximum(owner_col, 0)
+    for i, column in enumerate(
+        [code_col, prev_col, last_col, arrive_col, arrive_sib, owner_safe]
+    ):
         packed = jnp.where(lane_id == i, column, packed)
     tab_v[...] = packed
     tab_copy = pltpu.make_async_copy(tab_v, tab_s, tab_sem)
@@ -388,31 +395,26 @@
     for ring in rings:
         ring.first_far()
     for ring in rings:
-        ring.second_near(2, ring.near)
+        ring.second_near(2, ring.sides_c)
 
     scan[0, 0:16] = jnp.full((16, HEAD), NEGATIVE, F32)
     scan[0, 16:48] = jnp.zeros((32, HEAD), F32)
-    wait_bytes(q_all.at[pl.ds(0, n - 1)], recv_sem.at[1])
     token = lax.broadcasted_iota(jnp.int32, (16, PAGE), 1)
     for s in range(cap):
-        flat = jnp.maximum(tab_s[s, 0] - 1, 0)
-        present = tab_s[s, 0] > 0
-        owner = jnp.right_shift(flat, pages.bit_length() - 1)
-        page = jnp.bitwise_and(flat, pages - 1)
-        count = jnp.where(present, lengths_s[owner] - page * PAGE, 0)
-        product = lax.dot_general(
-            q_all[owner], kbuf[s], (((1,), (1,)), ((), ())), preferred_element_type=F32
-        )
-        scores[s] = jnp.where(token < count, product * SCALE, NEGATIVE)
+        kt[s] = kbuf[s].T
     for s in range(cap):
-        flat = jnp.maximum(tab_s[s, 0] - 1, 0)
-        present = tab_s[s, 0] > 0
-        owner = jnp.right_shift(flat, pages.bit_length() - 1)
-        page = jnp.bitwise_and(flat, pages - 1)
-        count = jnp.where(present, lengths_s[owner] - page * PAGE, 0)
+        code_s = tab_s[s, 0]
+        page = jnp.bitwise_and(jnp.maximum(code_s - 1, 0), pages - 1)
+        count = jnp.where(code_s > 0, lengths_s[tab_s[s, 5]] - page * PAGE, 0)
+        valid[s] = jnp.where(token < count, 1.0, 0.0)
+    wait_bytes(q_all.at[pl.ds(0, n - 1)], recv_sem.at[1])
+    for s in range(cap):
+        product = jnp.dot(q_all[tab_s[s, 5]], kt[s], preferred_element_type=F32)
+        scores[s] = jnp.where(valid[s] > 0.0, product * SCALE, NEGATIVE)
+    for s in range(cap):
         row = scores[s]
         top = jnp.max(row, axis=1, keepdims=True)
-        exact = jnp.where(token < count, jnp.exp(row - top), 0.0).astype(BF16)
+        exact = (jnp.exp(row - top) * valid[s]).astype(BF16)
         weights[s] = exact
         blocks[s, 0:16] = jnp.broadcast_to(top, (16, HEAD))
         blocks[s, 16:32] = jnp.broadcast_to(
@@ -443,9 +445,9 @@
         out_c[at] = scan[source, 32:48].astype(BF16)
         out_m[at, 0:1] = as_row(scan[source, 0:16], chosen)
         out_m[at, 1:2] = as_row(scan[source, 16:32], chosen)
-    for peer, at in peers:
-        remote(send_m.at[at], recv_m.at[at], 10, "ctx", peer).start()
-        remote(send_c.at[at], recv_c.at[at], 2, "ctx", peer).start()
+        if at:
+            remote(send_m.at[at], recv_m.at[at], 10, "ctx", peer).start()
+            remote(send_c.at[at], recv_c.at[at], 2, "ctx", peer).start()
     for ring in rings:
         ring.arrived(1)
         ring.second_near(3, ring.far)
@@ -676,6 +678,8 @@
             pltpu.VMEM((128, page_table.shape[1]), jnp.int32),
             pltpu.VMEM((rows_n, 128), jnp.int32),
             pltpu.SMEM((rows_n, 128), jnp.int32),
+            pltpu.VMEM((cap, HEAD, PAGE), BF16),
+            pltpu.VMEM((cap, 16, PAGE), F32),
             pltpu.VMEM((cap, 16, PAGE), F32),
             pltpu.VMEM((cap, 16, PAGE), BF16),
             pltpu.VMEM((cap, 48, HEAD), F32),

time: 40.5 us -> 39.6 us (0.978)
  Pallas kernels: 39.7 us -> 38.8 us
    pallas_call x1, Pallas kernels: 38.1 us -> 37.2 us  [per_device(): pl.pallas_call(functools.partial(kernel, n, tsize, (nx, ny, nc), depth *...]
where the time goes in v4:
time: 39.6 us; the launch traced here: 39.4 us
  Pallas kernels  38.8 us (98%)
  between operations  0.64 us (2%)
    pallas_call x1, Pallas kernels, per_device(): pl.pallas_call(functools.partial(kernel, n, tsize, (nx, ny, nc), depth *...  37.2 us
    pallas_call x1, Pallas kernels, per_device(): pl.pallas_call(store, out_shape=tuple((jax.ShapeDtypeStruct(o.shape, o.dt...  1.6 us

profile of v4, /device:TPU:1, one launch (start us, length us, event | category | flops | bytes accessed | tf_op | source)
XLA Modules:
  0.0 39.4 jit_solution(17233227905448607056)
XLA Ops:
  0.6 37.2 %decode_two_steps.1 = (bf16[4,256]{1,0:T(4,128)(2,1)S(1)}, bf16[4,256]{1,0:T(4,128)(2,1)S(1)}, bf16[43,128,128]{2,1,0:T(8,128)(2,1)S(1)}, bf16[43,128,128]{2,1,0:T(8,128)(2,1)S(1)}) custom-call(s32[32]{0:T(128)} %lengths_hbm.1, s32[64]{0:T(128)} %from_hbm.1, s32[64]{0:T(128)} %to_hbm.1, s32[32,128]{1,0:T(8,128)} %table_hbm.1, bf16[32,256]{1,0:T(8,128)(2,1)} %x1_hbm.1, ...), custom_call_target="tpu_custom_call" | custom-call | tf_op jit(solution)/shard_map/decode_two_steps/pallas_call | solution.py:648
  37.8 1.6 %store_results.1 = (bf16[4,256]{1,0:T(4,128)(2,1)}, bf16[4,256]{1,0:T(4,128)(2,1)}, bf16[43,128,128]{2,1,0:T(8,128)(2,1)}, bf16[43,128,128]{2,1,0:T(8,128)(2,1)}) custom-call(bf16[4,256]{1,0:T(4,128)(2,1)S(1)} %get-tuple-element.8.refs_0_, bf16[4,256]{1,0:T(4,128)(2,1)S(1)} %get-tuple-element.9.refs_1_, bf16[43,128,128]{2,1,0:T(8,128)(2,1)S(1)} %get-tuple-element.10.refs_2_, ...), custom_call_target="tpu_custom_call" | custom-call | tf_op jit(solution)/shard_map/store_results/pallas_call | solution.py:739

commit v5 on v4

--- a/solution.py
+++ b/solution.py
@@ -666,8 +666,8 @@
             pltpu.VMEM(w_query.shape, BF16),
             pltpu.VMEM(key_value_weight.shape, BF16),
             pltpu.VMEM(w_out.shape, BF16),
-            pltpu.VMEM((n * 16, HEAD), F32),
-            pltpu.VMEM((n * 8, HEAD), F32),
+            pltpu.VMEM((n * 16 + 16, HEAD), F32),
+            pltpu.VMEM((n * 8 + 8, HEAD), F32),
             pltpu.VMEM((n, 1, HEAD), F32),
             pltpu.VMEM((n, 1, HEAD), F32),
             pltpu.VMEM((n, 4, HEAD), F32),
@@ -689,7 +689,7 @@
             pltpu.VMEM((n, 2, HEAD), F32),
             pltpu.VMEM((n, 2, HEAD), F32),
             pltpu.VMEM((n, 16, HEAD), BF16),
-            pltpu.VMEM((n * 16, HEAD), F32),
+            pltpu.VMEM((n * 16 + 16, HEAD), F32),
             pltpu.VMEM((tsize, 4 * rows_t, depth // 2), F32),
             pltpu.VMEM((tsize, 4 * rows_t, depth // 2), BF16),
             pltpu.VMEM((tsize, 4 * rows_t, depth // 2), BF16),

time: 39.6 us -> 39.6 us (level)
  no operation moved by 1% of the time
where the time goes in v5:
time: 39.6 us; the launch traced here: 39.4 us
  Pallas kernels  38.8 us (98%)
  between operations  0.64 us (2%)
    pallas_call x1, Pallas kernels, per_device(): pl.pallas_call(functools.partial(kernel, n, tsize, (nx, ny, nc), depth *...  37.2 us
    pallas_call x1, Pallas kernels, per_device(): pl.pallas_call(store, out_shape=tuple((jax.ShapeDtypeStruct(o.shape, o.dt...  1.6 us

profile of v5, /device:TPU:1, one launch (start us, length us, event | category | flops | bytes accessed | tf_op | source)
XLA Modules:
  0.0 39.4 jit_solution(8584742689702377987)
XLA Ops:
  0.6 37.2 %decode_two_steps.1 = (bf16[4,256]{1,0:T(4,128)(2,1)S(1)}, bf16[4,256]{1,0:T(4,128)(2,1)S(1)}, bf16[43,128,128]{2,1,0:T(8,128)(2,1)S(1)}, bf16[43,128,128]{2,1,0:T(8,128)(2,1)S(1)}) custom-call(s32[32]{0:T(128)} %lengths_hbm.1, s32[64]{0:T(128)} %from_hbm.1, s32[64]{0:T(128)} %to_hbm.1, s32[32,128]{1,0:T(8,128)} %table_hbm.1, bf16[32,256]{1,0:T(8,128)(2,1)} %x1_hbm.1, ...), custom_call_target="tpu_custom_call" | custom-call | tf_op jit(solution)/shard_map/decode_two_steps/pallas_call | solution.py:648
  37.8 1.6 %store_results.1 = (bf16[4,256]{1,0:T(4,128)(2,1)}, bf16[4,256]{1,0:T(4,128)(2,1)}, bf16[43,128,128]{2,1,0:T(8,128)(2,1)}, bf16[43,128,128]{2,1,0:T(8,128)(2,1)}) custom-call(bf16[4,256]{1,0:T(4,128)(2,1)S(1)} %get-tuple-element.8.refs_0_, bf16[4,256]{1,0:T(4,128)(2,1)S(1)} %get-tuple-element.9.refs_1_, bf16[43,128,128]{2,1,0:T(8,128)(2,1)S(1)} %get-tuple-element.10.refs_2_, ...), custom_call_target="tpu_custom_call" | custom-call | tf_op jit(solution)/shard_map/store_results/pallas_call | solution.py:739
